TPU v7x, 512 devices: a whole 4x8x8 slice. The times are simulated.
512 devices in a mesh: row: 32 (over y, x), layer: 16 (over z, core).
Axes of the slice: x: 4, y: 8, z: 8, core: 2. Of those that a mesh axis runs over, the one named last changes fastest.
Arguments:
- panel_left: bfloat16 [32, 32, 2048, 128], P('row', 'layer'), may hold values from -6 to 6
- panel_right: bfloat16 [32, 32, 2048, 128], P('row', 'layer'), may hold values from -0.125 to 0.125
- test_matrix: bfloat16 [2048, 128], replicated, may hold values from -6 to 6
- ranks: int32 [32, 32], P('row', 'layer'), may hold values from 32 to 128, as said below
- offsets: int32 [32, 2], P('row'), may hold values from 1 to 4, as said below
Outputs:
- basis: float32 [32, 2048, 2, 128], P('row', 'layer')
- update_right: float32 [32, 2048, 2, 128], P('row', 'layer')
Inputs may be any that keep to these rules, and one draw needn't show every extreme that they name: `ranks`: some tile has rank 128 and some tile has rank 128 // 4. An owner's 2 offsets differ from each other; the values 1 and 4 occur in every draw.
All inputs are finite; a program needn't handle non-finite values.
Results may differ from a plain program's by a relative error of at most 0.0003.
Values may be sent and summed in bfloat16 or wider, within the bound.
A program may use at most 64 MiB of HBM per device.

v0:
```python
import jax
import jax.numpy as jnp
from jax import lax
from jax.sharding import PartitionSpec as P

FRONTS = 4
TARGETS = 2


def passed_along(x, axis, by):
    length = lax.axis_size(axis)
    return lax.ppermute(x, axis, [(i, (i + by) % length) for i in range(length)])


def constant_of(front_item):
    return lambda: front_item


def orthonormal(sketch_rows, gram_mat):
    factor = jnp.linalg.cholesky(gram_mat)
    by_cols = jnp.transpose(sketch_rows, (1, 2, 0))
    solved = lax.linalg.triangular_solve(factor, by_cols, left_side=True, lower=True)
    return jnp.transpose(solved, (2, 0, 1))


def gram_of(sketch_rows, tile_size):
    return (
        jnp.einsum("bsr,bsq->srq", sketch_rows, sketch_rows, precision=lax.Precision.HIGHEST)
        / tile_size
    )


def on_device(panel_left, panel_right, test_matrix, ranks, offsets):
    high = lax.Precision.HIGHEST
    tile_size = panel_left.shape[2]
    rank_cap = panel_left.shape[3]
    share_rows = tile_size // lax.axis_size("layer")
    columns = lax.broadcasted_iota(jnp.int32, (ranks.shape[1], 1, rank_cap), 2)
    live_cols = (columns < ranks[0][:, None, None]).astype(jnp.bfloat16)
    own_left = panel_left[0] * live_cols
    own_right = panel_right[0] * live_cols
    stacked = jnp.stack([own_left, own_right])
    fronts = []
    moving = stacked
    for step_no in range(FRONTS):
        moving = passed_along(moving, "row", 1)
        fronts.append(moving)
    branches = [constant_of(front_item) for front_item in fronts]
    left_full = own_left.astype(jnp.float32)
    cores = []
    mixers = []
    partners = []
    for target in range(TARGETS):
        partner = lax.switch(offsets[0, target] - 1, branches)
        core_mat = jnp.einsum(
            "kbr,kbq->krq", own_right, partner[1], preferred_element_type=jnp.float32
        )
        probes = jnp.einsum(
            "kbr,bq->krq", partner[0], test_matrix, preferred_element_type=jnp.float32
        )
        mix_mat = jnp.einsum("krq,kqs->krs", core_mat, probes, precision=high)
        cores.append(core_mat)
        mixers.append(mix_mat)
        partners.append(partner[0].astype(jnp.float32))
    mixed = jnp.stack(mixers, axis=1)
    local_sketch = jnp.einsum("kbr,ksrq->bsq", left_full, mixed, precision=high)
    total_sketch = lax.psum(local_sketch, "layer")
    basis_all = orthonormal(total_sketch, gram_of(total_sketch, tile_size))
    first_own = lax.axis_index("layer") * share_rows
    basis_part = lax.dynamic_slice_in_dim(basis_all, first_own, share_rows, 0)
    reach = jnp.einsum("kbr,bsq->ksrq", left_full, basis_all, precision=high)
    weights = []
    for target in range(TARGETS):
        weight_mat = jnp.einsum("krq,krs->kqs", cores[target], reach[:, target], precision=high)
        weights.append(weight_mat)
    term_list = []
    for target in range(TARGETS):
        row_piece = lax.slice_in_dim(
            partners[target], 0, share_rows * lax.axis_size("layer"), axis=1
        )
        term_list.append(jnp.einsum("kbq,kqs->bs", row_piece, weights[target], precision=high))
    update_right = lax.psum_scatter(
        jnp.stack(term_list, axis=1) / tile_size, "layer", scatter_dimension=0, tiled=True
    )
    return (basis_part[None], update_right[None])


def solution(mesh):
    return jax.shard_map(
        on_device,
        mesh=mesh,
        in_specs=(
            P("row", "layer", None, None),
            P("row", "layer", None, None),
            P(),
            P("row", "layer"),
            P("row", None),
        ),
        out_specs=(P("row", "layer", None, None), P("row", "layer", None, None)),
        check_vma=False,
    )
```

profile of v0, /device:TPU:6, one launch (start us, length us, event | category | flops | bytes accessed | tf_op | source)
XLA Modules:
  0.0 479.8 jit_solution(14630520279900826652)
XLA Ops:
  7.2 0.8 compare_convert_fusion
  8.0 1.7 broadcast_multiply_fusion.1
  9.9 3.4 collective-permute-start
  13.3 45.9 %collective-permute-done = bf16[2,2,2048,128]{3,2,1,0:T(8,128)(2,1)S(1)} collective-permute-done((bf16[2,2,2048,128]{3,2,1,0:T(8,128)(2,1)S(1)}, bf16[2,2,2048,128]{3,2,1,0:T(8,128)(2,1)S(1)}, u32[]{:S(2)}, u32[]{:S(2)}) %collective-permute-start) | collective-permute-done | bytes 2097184 | tf_op jit(solution)/shard_map/ppermute | solution.py:12
  59.2 5.5 %collective-permute-start.1 = (bf16[2,2,2048,128]{3,2,1,0:T(8,128)(2,1)S(1)}, bf16[2,2,2048,128]{3,2,1,0:T(8,128)(2,1)S(1)}, u32[]{:S(2)}, u32[]{:S(2)}) collective-permute-start(bf16[2,2,2048,128]{3,2,1,0:T(8,128)(2,1)S(1)} %collective-permute-done), channel_id=1, source_target_pairs={{0,16},{16,32},{32,48},{48,64},{64,80},{80,96},{96,112},{112,128},... | collective-permute-start | bytes 6291464 | tf_op jit(solution)/shard_map/ppermute | solution.py:12
  64.7 44.0 %collective-permute-done.1 = bf16[2,2,2048,128]{3,2,1,0:T(8,128)(2,1)S(1)} collective-permute-done((bf16[2,2,2048,128]{3,2,1,0:T(8,128)(2,1)S(1)}, bf16[2,2,2048,128]{3,2,1,0:T(8,128)(2,1)S(1)}, u32[]{:S(2)}, u32[]{:S(2)}) %collective-permute-start.1) | collective-permute-done | bytes 2097184 | tf_op jit(solution)/shard_map/ppermute | solution.py:12
  108.7 6.5 %collective-permute-start.2 = (bf16[2,2,2048,128]{3,2,1,0:T(8,128)(2,1)S(1)}, bf16[2,2,2048,128]{3,2,1,0:T(8,128)(2,1)}, u32[]{:S(2)}, u32[]{:S(2)}) collective-permute-start(bf16[2,2,2048,128]{3,2,1,0:T(8,128)(2,1)S(1)} %collective-permute-done.1), channel_id=1, source_target_pairs={{0,16},{16,32},{32,48},{48,64},{64,80},{80,96},{96,112},{112,128},... | collective-permute-start | bytes 6291464 | tf_op jit(solution)/shard_map/ppermute | solution.py:12
  115.2 43.1 %collective-permute-done.2 = bf16[2,2,2048,128]{3,2,1,0:T(8,128)(2,1)} collective-permute-done((bf16[2,2,2048,128]{3,2,1,0:T(8,128)(2,1)S(1)}, bf16[2,2,2048,128]{3,2,1,0:T(8,128)(2,1)}, u32[]{:S(2)}, u32[]{:S(2)}) %collective-permute-start.2) | collective-permute-done | bytes 2097184 | tf_op jit(solution)/shard_map/ppermute | solution.py:12
  158.2 6.6 %collective-permute-start.3 = (bf16[2,2,2048,128]{3,2,1,0:T(8,128)(2,1)}, bf16[2,2,2048,128]{3,2,1,0:T(8,128)(2,1)}, u32[]{:S(2)}, u32[]{:S(2)}) collective-permute-start(bf16[2,2,2048,128]{3,2,1,0:T(8,128)(2,1)} %collective-permute-done.2), channel_id=1, source_target_pairs={{0,16},{16,32},{32,48},{48,64},{64,80},{80,96},{96,112},{112,128},... | collective-permute-start | bytes 6291464 | tf_op jit(solution)/shard_map/ppermute | solution.py:12
  164.8 0.6 fusion.27
  166.7 40.6 %collective-permute-done.3 = bf16[2,2,2048,128]{3,2,1,0:T(8,128)(2,1)} collective-permute-done((bf16[2,2,2048,128]{3,2,1,0:T(8,128)(2,1)}, bf16[2,2,2048,128]{3,2,1,0:T(8,128)(2,1)}, u32[]{:S(2)}, u32[]{:S(2)}) %collective-permute-start.3) | collective-permute-done | bytes 2097184 | tf_op jit(solution)/shard_map/ppermute | solution.py:12
  207.3 3.1 conditional.2
  207.3 3.1 copy.37
  210.4 2.0 fusion.8
  212.4 3.1 conditional.3
  212.4 3.1 copy.32
  215.5 2.2 fusion.7
  218.4 0.5 fusion.12
  219.4 2.3 convolution_bitcast_fusion
  222.0 129.5 %all-reduce.2.cloned.1.call-done = f32[2048,2,128]{2,0,1:T(8,128)} async-done(((f32[2048,2,128]{2,0,1:T(8,128)}), f32[2048,2,128]{2,0,1:T(8,128)}) %all-reduce.2.cloned.1.call-update) | async-done | bytes 2097168 | tf_op jit(solution)/shard_map/psum | solution.py:67
  351.5 5.8 %fusion.28 = f32[2,128,128]{2,1,0:T(8,128)S(1)} fusion(f32[2048,2,128]{2,0,1:T(8,128)} %all-reduce.2.cloned.1.call-done), kind=kOutput, calls=%fused_computation.51 | convolution fusion | flops 805306368 | bytes 2228224 | tf_op jit(solution)/shard_map/bsr,bsq->srq/dot_general | solution.py:28
  357.5 23.5 %custom-call.7 = f32[2,128,128]{2,1,0:T(8,128)S(1)} custom-call(f32[2,128,128]{2,1,0:T(8,128)S(1)} %fusion.25), custom_call_target="Cholesky" | custom-call | tf_op jit(solution)/shard_map/jit(cholesky)/cholesky | solution.py:20
  381.2 19.9 %custom-call.8 = f32[2,1,128,128]{2,3,1,0:T(8,128)S(1)} custom-call(f32[2,1,128,128]{3,2,1,0:T(8,128)S(1)} %select_bitcast_fusion), custom_call_target="InvertDiagBlocksLowerTriangular" | custom-call | tf_op jit(solution)/shard_map/triangular_solve | solution.py:22
  401.1 2.0 fusion.2
  403.1 1.2 fusion.4
  405.4 1.0 convolution_bitcast_fusion.1
  406.4 1.0 convolution_bitcast_fusion.2
  407.5 1.4 maximum_multiply_fusion
  408.9 0.9 dynamic-slice_bitcast_fusion
  409.9 0.8 copy.21
  410.6 60.7 %reduce-scatter.2.cloned.1.call-done = f32[128,2,128]{2,0,1:T(8,128)} async-done(((f32[2048,2,128]{2,0,1:T(8,128)}), f32[128,2,128]{2,0,1:T(8,128)}) %reduce-scatter.2.cloned.1.call-update) | async-done | bytes 131088 | tf_op jit(solution)/shard_map/reduce_scatter | solution.py:82
  471.3 1.7 copy.22
  (39 shorter events, 3.2 us)
Async XLA Ops:
  7.2 210.5 %copy-start = (bf16[2048,128]{1,0:T(8,128)(2,1)S(1)}, bf16[2048,128]{1,0:T(8,128)(2,1)}, u32[]{:S(2)}) copy-start(bf16[2048,128]{1,0:T(8,128)(2,1)} %param.15) | copy-start | bytes 1572868
  7.2 344.3 %all-reduce.2.cloned.1.call-start = ((), (), s32[]{:S(2)}) async-start(), calls=%async_computation.1 | async-start | bytes 4194304 | tf_op jit(solution)/shard_map/psum | solution.py:67
  9.7 155.2 %copy-start.10 = (s32[1,2]{1,0:T(1,128)S(1)}, s32[1,2]{1,0:T(1,128)}, u32[]{:S(2)}) copy-start(s32[1,2]{1,0:T(1,128)} %param.17) | copy-start | bytes 28
  9.9 49.3 %collective-permute-start = (bf16[2,2,2048,128]{3,2,1,0:T(8,128)(2,1)S(1)}, bf16[2,2,2048,128]{3,2,1,0:T(8,128)(2,1)S(1)}, u32[]{:S(2)}, u32[]{:S(2)}) collective-permute-start(bf16[2,2,2048,128]{3,2,1,0:T(8,128)(2,1)S(1)} %pad_maximum_fusion), channel_id=1, source_target_pairs={{0,16},{16,32},{32,48},{48,64},{64,80},{80,96},{96,112},{112,128},... | collective-permute-start | bytes 6291464 | tf_op jit(solution)/shard_map/ppermute | solution.py:12
  59.2 148.1 %copy-start.5 = (bf16[2,2,2048,128]{3,2,1,0:T(8,128)(2,1)}, bf16[2,2,2048,128]{3,2,1,0:T(8,128)(2,1)S(1)}, u32[]{:S(2)}) copy-start(bf16[2,2,2048,128]{3,2,1,0:T(8,128)(2,1)S(1)} %collective-permute-done) | copy-start | bytes 6291460
  59.2 49.5 %collective-permute-start.1 = (bf16[2,2,2048,128]{3,2,1,0:T(8,128)(2,1)S(1)}, bf16[2,2,2048,128]{3,2,1,0:T(8,128)(2,1)S(1)}, u32[]{:S(2)}, u32[]{:S(2)}) collective-permute-start(bf16[2,2,2048,128]{3,2,1,0:T(8,128)(2,1)S(1)} %collective-permute-done), channel_id=1, source_target_pairs={{0,16},{16,32},{32,48},{48,64},{64,80},{80,96},{96,112},{112,128},... | collective-permute-start | bytes 6291464 | tf_op jit(solution)/shard_map/ppermute | solution.py:12
  108.7 49.6 %collective-permute-start.2 = (bf16[2,2,2048,128]{3,2,1,0:T(8,128)(2,1)S(1)}, bf16[2,2,2048,128]{3,2,1,0:T(8,128)(2,1)}, u32[]{:S(2)}, u32[]{:S(2)}) collective-permute-start(bf16[2,2,2048,128]{3,2,1,0:T(8,128)(2,1)S(1)} %collective-permute-done.1), channel_id=1, source_target_pairs={{0,16},{16,32},{32,48},{48,64},{64,80},{80,96},{96,112},{112,128},... | collective-permute-start | bytes 6291464 | tf_op jit(solution)/shard_map/ppermute | solution.py:12
  158.2 49.1 %collective-permute-start.3 = (bf16[2,2,2048,128]{3,2,1,0:T(8,128)(2,1)}, bf16[2,2,2048,128]{3,2,1,0:T(8,128)(2,1)}, u32[]{:S(2)}, u32[]{:S(2)}) collective-permute-start(bf16[2,2,2048,128]{3,2,1,0:T(8,128)(2,1)} %collective-permute-done.2), channel_id=1, source_target_pairs={{0,16},{16,32},{32,48},{48,64},{64,80},{80,96},{96,112},{112,128},... | collective-permute-start | bytes 6291464 | tf_op jit(solution)/shard_map/ppermute | solution.py:12
  215.5 2.2 copy-start.8
  215.5 2.9 copy-start.6
  217.7 1.7 copy-start.2
  221.8 249.6 %reduce-scatter.2.cloned.1.call-start = ((), (), s32[]{:S(2)}) async-start(), calls=%async_computation.2 | async-start | bytes 2228224 | tf_op jit(solution)/shard_map/reduce_scatter | solution.py:82
  351.5 49.6 %copy-start.1 = (f32[2048,2,128]{2,0,1:T(8,128)S(1)}, f32[2048,2,128]{2,0,1:T(8,128)}, u32[]{:S(2)}) copy-start(f32[2048,2,128]{2,0,1:T(8,128)} %all-reduce.2.cloned.1.call-done) | copy-start | bytes 6291460
  401.1 2.0 copy-start.3
  403.1 2.0 copy-start.4
  403.1 2.3 copy-start.7
  404.3 2.1 copy-start.9
Sparse Core Ops, SparseCore 0:
  221.9 129.5 all-reduce.1
  409.0 62.2 reduce-scatter.1
where the time goes:
time: 480 us
  waiting for transfers between devices  364 us (76%)
  other arithmetic  47.7 us (10%)
  starting transfers between devices  22.2 us (5%)
  matrix products  19.8 us (4%)
  between operations  15.6 us (3%)
  local copies, waits for them, and re-layouts  10.7 us (2%)
    ppermute x4, waiting for transfers between devices, passed_along(): lax.ppermute(x, axis, [(i, (i + by) % length) for i in range(length)])  173 us
    psum x1, waiting for transfers between devices, on_device(): total_sketch = lax.psum(local_sketch, 'layer')  129 us
    reduce_scatter x1, waiting for transfers between devices, on_device(): lax.psum_scatter(jnp.stack(term_list, axis=1) / tile_size, 'layer', scatt...  60.7 us
    another operation x4, other arithmetic, orthonormal(): factor = jnp.linalg.cholesky(gram_mat)  23.6 us
    ppermute x4, starting transfers between devices, passed_along(): lax.ppermute(x, axis, [(i, (i + by) % length) for i in range(length)])  22 us
    another operation x3, other arithmetic, orthonormal(): lax.linalg.triangular_solve(factor, by_cols, left_side=True, lower=True)  20 us
  transfers between devices with their start and end apart: 6, of which 6 were waited for; matrix products, arithmetic and copies ran while one was open for 0% of the time, Pallas kernels for 0%

commit v1 on v0

v1 whole, which is shorter than its diff:
```python
import functools

import jax
import jax.numpy as jnp
from jax import lax
from jax.experimental import pallas as pl
from jax.experimental.pallas import tpu as pltpu
from jax.sharding import PartitionSpec as P

R = 128
X = 4
FRONTS = 4
TARGETS = 2
BF = jnp.bfloat16
F32 = jnp.float32
HIGH = lax.Precision.HIGHEST


def dot(a, b, ca=1, cb=0, precision=None):
    return lax.dot_general(
        a, b, (((ca,), (cb,)), ((), ())), precision=precision, preferred_element_type=F32
    )


def split(a):
    high = a.astype(BF)
    return high, (a - high.astype(F32)).astype(BF)


def kernel(
    rows, layers, tile,
    u_ref, v_ref, test_ref, ranks_ref, offs_ref,
    basis_ref, upd_ref,
    un, um, vm, vq, uq, usel, meta, metas, probe_own, probes, parts, chain_in, plain_in, sum_out, sum_in, core,
    mix, s_part, s_cx, s_send, s_recv, s_own, s_full, gx, linv, reach, wall, t_part, t_cx, t_send, t_recv, t_own, t_fin,
    a2v_s, a2v_r, a2u_s, a2u_r, yv_s, yv_r, yu_s, yu_r, mt_s, mt_r, pr_s, pr_r, cr_s, cr_r,
    scx_s, scx_r, srs_s, srs_r, ag_s, ag_r, agc_s, agc_r, wg_s, wg_r, tcx_s, tcx_r, trs_s, trs_r, fin_s, fin_r,
):
    ny, nz = rows // X, layers // 2
    np_, nm = nz // 2, nz - 1 - nz // 2
    br = tile // layers
    qr, hb = br // X, br // 2
    quarter = tile // X
    row, layer = lax.axis_index("row"), lax.axis_index("layer")
    x, y = lax.rem(row, X), lax.div(row, X)
    z, c = lax.div(layer, 2), lax.rem(layer, 2)

    def xdev(d):
        return (y * X + lax.rem(x + d, X), layer)

    def ydev(d):
        return (lax.rem(y + d + ny, ny) * X + x, layer)

    def zdev(d):
        return (row, lax.rem(z + d + nz, nz) * 2 + c)

    mate = (row, z * 2 + 1 - c)
    barrier = pltpu.get_barrier_semaphore()
    friends = [xdev(1), xdev(2), xdev(3), ydev(1), ydev(-1), zdev(1), zdev(-1), mate]
    for friend in friends:
        pl.semaphore_signal(barrier, inc=1, device_id=friend, device_id_type=pl.DeviceIdType.MESH)

    def remote(src, dst, ssem, rsem, dev):
        return pltpu.make_async_remote_copy(
            src_ref=src, dst_ref=dst, send_sem=ssem, recv_sem=rsem,
            device_id=dev, device_id_type=pl.DeviceIdType.MESH,
        )

    pending = []

    def start(copy):
        copy.start()
        pending.append(copy)
        return copy

    lanes = lax.broadcasted_iota(jnp.int32, (1, R), 1)
    live = [(lanes < ranks_ref[0, k]).astype(F32).astype(BF) for k in range(2)]

    def mask_rows(i, carry):
        src = pl.ds(pl.multiple_of(i * br, br), br)
        for k in range(2):
            v = v_ref[0, k, src, :] * live[k]
            for xx in range(X):
                vm[xx, k, pl.ds(pl.multiple_of(i * qr, qr), qr), :] = v[xx * qr:(xx + 1) * qr]
        return carry

    lax.fori_loop(0, layers, mask_rows, 0)
    vq[X + x] = vm[x]
    for s in range(TARGETS):
        meta[s, :, :] = jnp.full((8, R), offs_ref[0, s], jnp.int32).astype(F32)
    metas[x] = meta[...]
    pl.semaphore_wait(barrier, len(friends))

    def slot_of(d):
        return lax.rem(x - d + X, X)

    def a2a(d, src, dst, ss, rs):
        return remote(src.at[lax.rem(x + d, X)], dst.at[X + x], ss.at[d], rs.at[d], xdev(d))

    def ysend(d, buf, ss, rs):
        return remote(buf.at[X + slot_of(d)], buf.at[slot_of(d)], ss.at[d], rs.at[d], ydev(1))

    yv = [ysend(d, vq, yv_s, yv_r) for d in range(X)]
    start(yv[0])
    av = {d: start(a2a(d, vm, vq, a2v_s, a2v_r)) for d in (2, 1, 3)}
    mts = {d: start(remote(meta, metas.at[x], mt_s.at[d], mt_r.at[d], xdev(d))) for d in (1, 2, 3)}

    def mask_left(i, carry):
        src = pl.ds(pl.multiple_of(i * br, br), br)
        for k in range(2):
            u = u_ref[0, k, src, :] * live[k]
            un[k, src, :] = u
            for xx in range(X):
                um[xx, k, pl.ds(pl.multiple_of(i * qr, qr), qr), :] = u[xx * qr:(xx + 1) * qr]
        return carry

    lax.fori_loop(0, layers, mask_left, 0)
    uq[X + x] = um[x]
    for k in range(2):
        probe_own[k] = jnp.zeros((R, R), F32)

    def probe_rows(i, carry):
        src = pl.ds(pl.multiple_of(i * br, br), br)
        for k in range(2):
            probe_own[k] += dot(un[k, src, :], test_ref[src, :], 0, 0)
        return carry

    lax.fori_loop(0, layers, probe_rows, 0)
    pry = start(remote(probe_own, probes.at[FRONTS - 1], pr_s.at[0], pr_r.at[0], ydev(1)))
    for d in (1, 3, 2):
        av[d].wait_recv()
        start(yv[d])

    def probe_send(d, src):
        return remote(src, probes.at[d - 1], pr_s.at[d], pr_r.at[d], xdev(d))

    for d in (1, 2, 3):
        @pl.when(x + d < X)
        def _(d=d):
            probe_send(d, probe_own).start()
    pry.wait_recv()
    for d in (1, 2, 3):
        @pl.when(x + d >= X)
        def _(d=d):
            probe_send(d, probes.at[FRONTS - 1]).start()
    prx = [probe_send(d, probe_own) for d in (1, 2, 3)]
    pending.extend(prx)
    for copy in mts.values():
        copy.wait_recv()
    for d in range(X):
        yv[d].wait_recv()

    yu = [ysend(d, uq, yu_s, yu_r) for d in range(X)]
    start(yu[0])

    picks = [[[(metas[xx, s, 0:1, :] == o).astype(F32) for o in range(1, FRONTS + 1)]
              for s in range(TARGETS)] for xx in range(X)]

    for xx in range(X):
        for k in range(2):
            mine = vq[X + xx, k]
            found = [dot(mine, vq[X + xx - o, k], 0, 0) for o in range(1, FRONTS + 1)]
            for s in range(TARGETS):
                total = found[0] * picks[xx][s][0]
                for o in range(1, FRONTS):
                    total = total + found[o] * picks[xx][s][o]
                parts[xx, s, k] = total

    far = lax.rem(x + 2, X)
    right, left = lax.rem(x + 1, X), lax.rem(x + 3, X)
    far0 = start(remote(parts.at[far, 0], chain_in.at[0], cr_s.at[0], cr_r.at[0], xdev(3)))
    far1 = start(remote(parts.at[far, 1], chain_in.at[1], cr_s.at[1], cr_r.at[1], xdev(1)))
    plain0 = start(remote(parts.at[right, 0], plain_in.at[0], cr_s.at[2], cr_r.at[2], xdev(1)))
    plain1 = start(remote(parts.at[left, 1], plain_in.at[1], cr_s.at[3], cr_r.at[3], xdev(3)))
    far0.wait_recv()
    sum_out[0] = parts[left, 0] + chain_in[0]
    sum0 = start(remote(sum_out.at[0], sum_in.at[0], cr_s.at[4], cr_r.at[4], xdev(3)))
    far1.wait_recv()
    sum_out[1] = parts[right, 1] + chain_in[1]
    sum1 = start(remote(sum_out.at[1], sum_in.at[1], cr_s.at[5], cr_r.at[5], xdev(1)))
    for copy in prx:
        copy.wait_recv()
    plain0.wait_recv()
    plain1.wait_recv()
    sum0.wait_recv()
    sum1.wait_recv()
    for s in range(TARGETS):
        core[s] = parts[x, s] + plain_in[s] + sum_in[s]

    au = {d: start(a2a(d, um, uq, a2u_s, a2u_r)) for d in (2, 1, 3)}

    for s in range(TARGETS):
        for k in range(2):
            back = jnp.clip(offs_ref[0, s] - 1, 0, FRONTS - 1)
            mixed = dot(core[s, k], probes[back, k], precision=HIGH)
            high, low = split(mixed)
            mix[0, k * R:(k + 1) * R, s * R:(s + 1) * R] = high
            mix[1, k * R:(k + 1) * R, s * R:(s + 1) * R] = low

    def order(i):
        half = lax.div(i + 1, 2)
        off = jnp.where(lax.rem(i, 2) == 1, half - np_, np_ - half)
        return lax.rem(z + off + nz, nz)

    def pair_copy(part, cx, ss, rs, zz):
        return remote(part.at[1 - c, zz], cx.at[zz], ss.at[zz], rs.at[zz], mate)

    def sketch_rows(i, carry):
        zz = order(i)
        for other in (1, 0):
            par = 1 - c if other else c
            src = pl.ds(pl.multiple_of((zz * 2 + par) * br, br), br)
            both = jnp.concatenate([un[0, src, :], un[1, src, :]], axis=1)
            s_part[par, zz] = dot(both, mix[0]) + dot(both, mix[1])
            if other:
                pair_copy(s_part, s_cx, scx_s, scx_r, zz).start()
        return carry

    lax.fori_loop(0, nz, sketch_rows, 0)

    chains = [(1, 0, np_), (-1, 0, nm), (1, 1, nm), (-1, 1, np_)]

    def ring_reduce(part, cx, send, recv, ss_cx, rs_cx, ss, rs, own, between):
        waited = set()

        def term(off, h):
            zz = lax.rem(z + off + 2 * nz, nz)
            if off % nz not in waited:
                waited.add(off % nz)
                pair_copy(part, cx, ss_cx, rs_cx, zz).wait_recv()
            at = pl.ds(h * hb, hb)
            return part[c, zz, at, :] + cx[zz, at, :]

        def hop(ch, i):
            return remote(send.at[ch, i], recv.at[ch, i], ss.at[ch, i], rs.at[ch, i], zdev(chains[ch][0]))

        for i in range(np_):
            for ch, (sgn, h, n) in enumerate(chains):
                j = i - (np_ - n)
                if j < 0:
                    continue
                value = term(sgn * (n - j), h)
                if j > 0:
                    hop(ch, j - 1).wait_recv()
                    value = value + recv[ch, j - 1]
                send[ch, j] = value
                start(hop(ch, j))
            between(i)
        for h in range(2):
            value = term(0, h)
            for ch, (sgn, hh, n) in enumerate(chains):
                if hh == h and n > 0:
                    hop(ch, n - 1).wait_recv()
                    value = value + recv[ch, n - 1]
            own[h * hb:(h + 1) * hb, :] = value

    def forward_left(i):
        for d in {0: (1,), 1: (3,), 2: (2,)}.get(i, ()):
            au[d].wait_recv()
            start(yu[d])

    if np_ >= 3:
        ring_reduce(s_part, s_cx, s_send, s_recv, scx_s, scx_r, srs_s, srs_r, s_own, forward_left)
    else:
        ring_reduce(s_part, s_cx, s_send, s_recv, scx_s, scx_r, srs_s, srs_r, s_own, lambda i: None)
        for i in range(3):
            forward_left(i)

    high, low = split(s_own[...])
    for h in range(2):
        s_full[c, z, h, 0] = high[h * hb:(h + 1) * hb]
        s_full[c, z, h, 1] = low[h * hb:(h + 1) * hb]

    def gather_hop(ch, i):
        sgn, h, n = chains[ch]
        zz = lax.rem(z - sgn * i + nz, nz)
        return remote(s_full.at[c, zz, h], s_full.at[c, zz, h], ag_s.at[ch, i], ag_r.at[ch, i], zdev(sgn))

    def to_mate(off, h):
        zz = lax.rem(z + off + nz, nz)
        at = (off + nz) % nz
        return remote(s_full.at[c, zz, h], s_full.at[c, zz, h], agc_s.at[at, h], agc_r.at[at, h], mate)

    for ch, (sgn, h, n) in enumerate(chains):
        if n > 0:
            start(gather_hop(ch, 0))
    for h in range(2):
        start(to_mate(0, h))
    for i in range(np_):
        for ch, (sgn, h, n) in enumerate(chains):
            if i < n:
                gather_hop(ch, i).wait_recv()
                if i + 1 < n:
                    start(gather_hop(ch, i + 1))
                start(to_mate(-sgn * (i + 1), h))
    for off in range(nz):
        for h in range(2):
            to_mate(off, h).wait_recv()

    reach[...] = jnp.zeros_like(reach)
    gx[...] = jnp.zeros_like(gx)

    def reach_rows(zz, carry):
        src = pl.ds(pl.multiple_of(zz * 2 * br, 2 * br), 2 * br)
        both = jnp.concatenate([un[0, src, :], un[1, src, :]], axis=1)
        pieces = [(a, b) for a in range(2) for b in range(2)]
        shigh = jnp.concatenate([s_full[a, zz, b, 0] for a, b in pieces], axis=0)
        slow = jnp.concatenate([s_full[a, zz, b, 1] for a, b in pieces], axis=0)
        reach[...] += dot(both, shigh, 0, 0) + dot(both, slow, 0, 0)
        for s in range(TARGETS):
            at = slice(s * R, (s + 1) * R)
            gx[s, :, 0:R] += dot(shigh[:, at], shigh[:, at], 0, 0)
            gx[s, :, R:2 * R] += dot(shigh[:, at], slow[:, at], 0, 0)
        return carry

    lax.fori_loop(0, nz, reach_rows, 0)

    for s in range(TARGETS):
        for k in range(2):
            weight = dot(core[s, k], reach[k * R:(k + 1) * R, s * R:(s + 1) * R], 0, 0, precision=HIGH)
            high, low = split(weight)
            wall[x, s, k * R:(k + 1) * R, 0:R] = high
            wall[x, s, k * R:(k + 1) * R, R:2 * R] = low

    def weight_send(i, who, s, d):
        return remote(wall.at[who, s], wall.at[who, s], wg_s.at[i], wg_r.at[i], xdev(d))

    wr1 = start(weight_send(0, x, 1, 1))
    wl0 = start(weight_send(1, x, 0, 3))
    wr0 = start(weight_send(2, x, 0, 1))
    wl1 = start(weight_send(3, x, 1, 3))

    eye = (lax.broadcasted_iota(jnp.int32, (R, R), 0) == lax.broadcasted_iota(jnp.int32, (R, R), 1)).astype(F32)
    for s in range(TARGETS):
        cross = gx[s, :, R:2 * R]
        gx[s, :, 0:R] = (gx[s, :, 0:R] + (cross + cross.T)) / tile
        gx[s, :, R:2 * R] = eye

    lane8 = lax.broadcasted_iota(jnp.int32, (8, R), 1)
    sub8 = lax.broadcasted_iota(jnp.int32, (8, R), 0)

    def factor_block(b, carry):
        r0 = pl.multiple_of(b * 8, 8)
        for s in range(TARGETS):
            gg = gx[s, pl.ds(r0, 8), 0:R]
            xx = gx[s, pl.ds(r0, 8), R:2 * R]
            cols = [
                jnp.broadcast_to(
                    jnp.sum(jnp.where(lane8 == r0 + j, gg, 0.0), axis=1, keepdims=True), (8, R))
                for j in range(8)
            ]
            diag = jnp.ones((8, R), F32)
            for j in range(8):
                pivot = cols[j][j:j + 1]
                diag = jnp.where(sub8 == j, pivot, diag)
                f = jnp.where(sub8 > j, cols[j] / pivot, 0.0)
                for m in range(j + 1, 8):
                    cols[m] = cols[m] - f * cols[m][j:j + 1]
                gg = gg - f * gg[j:j + 1]
                xx = xx - f * xx[j:j + 1]
            linv[s, pl.ds(r0, 8), :] = xx / jnp.sqrt(diag)
            lead = jnp.where(lane8 >= r0 + 8, gg / diag, 0.0)
            gx[s, :, 0:R] -= dot(lead, gg, 0, 0, precision=HIGH)
            gx[s, :, R:2 * R] -= dot(lead, xx, 0, 0, precision=HIGH)
        return carry

    blocks = R // 8
    lax.fori_loop(0, blocks // 4, factor_block, 0)
    wr1.wait_recv()
    fr1 = start(weight_send(4, left, 1, 1))
    wl0.wait_recv()
    fl0 = start(weight_send(5, right, 0, 3))

    for d in range(X):
        yu[d].wait_recv()
    pick16 = [[[w.astype(BF) for w in picks[xx][s]] for s in range(TARGETS)] for xx in range(X)]

    def choose_rows(i, carry):
        src = pl.ds(pl.multiple_of(i * 32, 32), 32)
        for xx in range(X):
            for k in range(2):
                cand = [uq[X + xx - o, k, src, :] for o in range(1, FRONTS + 1)]
                for s in range(TARGETS):
                    total = cand[0] * pick16[xx][s][0]
                    for o in range(1, FRONTS):
                        total = total + cand[o] * pick16[xx][s][o]
                    usel[xx, s, src, k * R:(k + 1) * R] = total
        return carry

    lax.fori_loop(0, quarter // 32, choose_rows, 0)
    lax.fori_loop(blocks // 4, blocks // 2, factor_block, 0)
    for copy in (wr0, wl1, fr1, fl0):
        copy.wait_recv()

    def term_rows(q, carry):
        src = pl.ds(pl.multiple_of(q * 4 * qr, 4 * qr), 4 * qr)
        for xx in range(X):
            for s in range(TARGETS):
                got = dot(usel[xx, s, src, :], wall[xx, s])
                got = got[:, 0:R] + got[:, R:2 * R]
                for i in range(4):
                    t_part[i % 2, q * 2 + i // 2, xx * qr:(xx + 1) * qr, s * R:(s + 1) * R] = got[i * qr:(i + 1) * qr]
        return carry

    lax.fori_loop(0, layers // 4, term_rows, 0)

    def pair_start(i, carry):
        pair_copy(t_part, t_cx, tcx_s, tcx_r, order(i)).start()
        return carry

    lax.fori_loop(0, nz, pair_start, 0)
    rest = blocks // 2

    def factor_more(i):
        lax.fori_loop(rest + i * rest // np_, rest + (i + 1) * rest // np_, factor_block, 0)

    ring_reduce(t_part, t_cx, t_send, t_recv, tcx_s, tcx_r, trs_s, trs_r, t_own, factor_more)

    def final_send(d):
        at = pl.ds(pl.multiple_of(lax.rem(x + d, X) * qr, qr), qr)
        return remote(t_own.at[at, :], t_fin.at[x], fin_s.at[d], fin_r.at[d], xdev(d))

    fins = [start(final_send(d)) for d in (2, 1, 3)]
    t_fin[x] = t_own[pl.ds(pl.multiple_of(x * qr, qr), qr), :]
    for s in range(TARGETS):
        at = slice(s * R, (s + 1) * R)
        basis_ref[0, :, s, :] = dot(s_own[:, at], linv[s], 1, 1, precision=HIGH)
    for copy in fins:
        copy.wait_recv()
    for s in range(TARGETS):
        at = slice(s * R, (s + 1) * R)
        terms = jnp.concatenate([t_fin[i, :, at] for i in range(X)], axis=0)
        upd_ref[0, :, s, :] = dot(terms, linv[s], 1, 1, precision=HIGH) / tile

    for copy in pending:
        copy.wait_send()

    def pair_end(zz, carry):
        pair_copy(s_part, s_cx, scx_s, scx_r, zz).wait_send()
        pair_copy(t_part, t_cx, tcx_s, tcx_r, zz).wait_send()
        return carry

    lax.fori_loop(0, nz, pair_end, 0)


def on_device(panel_left, panel_right, test_matrix, ranks, offsets):
    rows, layers = lax.axis_size("row"), lax.axis_size("layer")
    tile = panel_left.shape[2]
    nz = layers // 2
    np_ = max(nz // 2, 1)
    br = tile // layers
    qr, hb, quarter = br // X, br // 2, tile // X
    dma = pltpu.SemaphoreType.DMA
    vmem = pltpu.VMEM
    ring = [
        vmem((2, nz, br, 2 * R), F32), vmem((nz, br, 2 * R), F32),
        vmem((4, np_, hb, 2 * R), F32), vmem((4, np_, hb, 2 * R), F32), vmem((br, 2 * R), F32),
    ]
    scratch = [
        vmem((2, tile, R), BF), vmem((X, 2, quarter, R), BF), vmem((X, 2, quarter, R), BF),
        vmem((2 * X, 2, quarter, R), BF), vmem((2 * X, 2, quarter, R), BF),
        vmem((X, TARGETS, quarter, 2 * R), BF),
        vmem((TARGETS, 8, R), F32), vmem((X, TARGETS, 8, R), F32),
        vmem((2, R, R), F32), vmem((FRONTS, 2, R, R), F32),
        vmem((X, TARGETS, 2, R, R), F32),
        vmem((TARGETS, 2, R, R), F32), vmem((TARGETS, 2, R, R), F32), vmem((TARGETS, 2, R, R), F32),
        vmem((TARGETS, 2, R, R), F32), vmem((TARGETS, 2, R, R), F32),
        vmem((2, 2 * R, 2 * R), BF),
        *ring,
        vmem((2, nz, 2, 2, hb, 2 * R), BF),
        vmem((TARGETS, R, 2 * R), F32), vmem((TARGETS, R, R), F32), vmem((2 * R, 2 * R), F32),
        vmem((X, TARGETS, 2 * R, 2 * R), BF),
        *ring,
        vmem((X, qr, 2 * R), F32),
        dma((X,)), dma((X,)), dma((X,)), dma((X,)), dma((X,)), dma((X,)), dma((X,)), dma((X,)),
        dma((X,)), dma((X,)), dma((X,)), dma((X,)), dma((6,)), dma((6,)),
        dma((nz,)), dma((nz,)), dma((4, np_)), dma((4, np_)),
        dma((4, np_)), dma((4, np_)), dma((nz, 2)), dma((nz, 2)),
        dma((6,)), dma((6,)),
        dma((nz,)), dma((nz,)), dma((4, np_)), dma((4, np_)),
        dma((X,)), dma((X,)),
    ]
    inside = pl.BlockSpec(memory_space=pltpu.VMEM)
    scalars = pl.BlockSpec(memory_space=pltpu.SMEM)
    out = jax.ShapeDtypeStruct((1, br, TARGETS, R), F32)
    return pl.pallas_call(
        functools.partial(kernel, rows, layers, tile),
        out_shape=(out, out),
        in_specs=[inside, inside, inside, scalars, scalars],
        out_specs=(inside, inside),
        scratch_shapes=scratch,
        compiler_params=pltpu.CompilerParams(
            collective_id=0, has_side_effects=True, vmem_limit_bytes=50 * 2**20
        ),
        name="trailing_update",
    )(panel_left, panel_right, test_matrix, ranks, offsets)


def solution(mesh):
    return jax.shard_map(
        on_device,
        mesh=mesh,
        in_specs=(
            P("row", "layer", None, None),
            P("row", "layer", None, None),
            P(),
            P("row", "layer"),
            P("row", None),
        ),
        out_specs=(P("row", "layer", None, None), P("row", "layer", None, None)),
        check_vma=False,
    )
```

time: 480 us -> 146 us (0.30)
  waiting for transfers between devices: 364 us -> 0 us
  Pallas kernels: 0 us -> 138 us
  other arithmetic: 47.7 us -> 0 us
  starting transfers between devices: 22.2 us -> 0 us
  matrix products: 19.8 us -> 0 us
  between operations: 15.6 us -> 0.65 us
    ppermute x4 -> x0, waiting for transfers between devices: 173 us -> none  [passed_along(): lax.ppermute(x, axis, [(i, (i + by) % length) for i in range(length)])]
    pallas_call x0 -> x1, Pallas kernels: none -> 138 us  [on_device(): pl.pallas_call(functools.partial(kernel, rows, layers, tile), out_shape=(...]
    psum x1 -> x0, waiting for transfers between devices: 129 us -> none  [on_device(): total_sketch = lax.psum(local_sketch, 'layer')]
    reduce_scatter x1 -> x0, waiting for transfers between devices: 60.7 us -> none  [on_device(): lax.psum_scatter(jnp.stack(term_list, axis=1) / tile_size, 'layer', scatt...]
    another operation x8 -> x0, other arithmetic: 43.8 us -> none  [the longest x4 23.6 us: orthonormal(): factor = jnp.linalg.cholesky(gram_mat)]
    ppermute x4 -> x0, starting transfers between devices: 22 us -> none  [passed_along(): lax.ppermute(x, axis, [(i, (i + by) % length) for i in range(length)])]
    dot_general x13 -> x0, matrix products: 17.8 us -> none  [the longest x1 5.81 us: gram_of(): jnp.einsum('bsr,bsq->srq', sketch_rows, sketch_rows, precision=lax.Precis...]
    cond x2 -> x0, local copies, waits for them, and re-layouts: 6.13 us -> none
  transfers between devices with their start and end apart: 6 -> 0, of which waited for: 6 -> 0; matrix products, arithmetic and copies ran while one was open for 0% -> 0% of each run, Pallas kernels for 0% -> 0%
where the time goes in v1:
time: 146 us; the launch traced here: 145 us
  Pallas kernels  138 us (95%)
  local copies, waits for them, and re-layouts  6.11 us (4%)
    pallas_call x1, Pallas kernels, on_device(): pl.pallas_call(functools.partial(kernel, rows, layers, tile), out_shape=(...  138 us
    unnamed x12, local copies, waits for them, and re-layouts  6.11 us

profile of v1, /device:TPU:6, one launch (start us, length us, event | category | flops | bytes accessed | tf_op | source)
XLA Modules:
  0.0 144.6 jit_solution(11645548396442647293)
XLA Ops:
  0.6 0.0 copy-start
  0.6 1.2 copy-done
  1.9 0.0 copy-start.1
  1.9 1.2 copy-done.1
  3.1 0.0 copy-start.2
  3.1 1.0 copy-done.2
  4.1 0.0 copy-start.3
  4.1 0.7 copy-done.3
  4.8 0.0 copy-start.4
  4.8 0.7 copy-done.4
  5.4 137.8 %trailing_update.1 = (f32[1,128,2,128]{3,2,1,0:T(2,128)S(1)}, f32[1,128,2,128]{3,2,1,0:T(2,128)S(1)}) custom-call(bf16[1,2,2048,128]{3,2,1,0:T(8,128)(2,1)S(1)} %copy-done, bf16[1,2,2048,128]{3,2,1,0:T(8,128)(2,1)S(1)} %copy-done.1, bf16[2048,128]{1,0:T(8,128)(2,1)S(1)} %copy-done.2, s32[1,2]{1,0:T(1,128)S(1)} %copy-done.3, s32[1,2]{1,0:T(1,128)S(1)} %copy-done.4), custom_call_target="tpu_custom_call" | custom-call | tf_op jit(solution)/shard_map/trailing_update/pallas_call | solution.py:486
  143.3 0.7 copy.9
  143.9 0.7 copy.10
Async XLA Ops:
  0.6 1.2 copy-start
  1.9 1.2 copy-start.1
  3.1 1.0 copy-start.2
  4.1 0.7 copy-start.3
  4.8 0.7 copy-start.4

commit v2 on v1

v2 whole, which is shorter than its diff:
```python
import functools

import jax
import jax.numpy as jnp
from jax import lax
from jax.experimental import pallas as pl
from jax.experimental.pallas import tpu as pltpu
from jax.sharding import PartitionSpec as P

R = 128
X = 4
FRONTS = 4
TARGETS = 2
BF = jnp.bfloat16
F32 = jnp.float32
HIGH = lax.Precision.HIGHEST


def dot(a, b, ca=1, cb=0, precision=None):
    return lax.dot_general(
        a, b, (((ca,), (cb,)), ((), ())), precision=precision, preferred_element_type=F32
    )


def split(a):
    high = a.astype(BF)
    return high, (a - high.astype(F32)).astype(BF)


EXTRA = 16
STEPS = 128.0
TOP = 32766.0


def coded(value, ref, *at):
    n = value.shape[0]
    most = jnp.maximum(jnp.max(jnp.abs(value), axis=0, keepdims=True), 1e-30)
    code = jnp.ceil(jnp.log2(most) * STEPS) + 1.0
    ref[(*at, slice(0, n), slice(None))] = (
        jnp.round(value * (TOP * jnp.exp2(code * (-1.0 / STEPS)))).astype(jnp.int32).astype(jnp.int16)
    )
    ref[(*at, slice(n, n + EXTRA), slice(None))] = (
        jnp.broadcast_to(code, (EXTRA, value.shape[1])).astype(jnp.int32).astype(jnp.int16)
    )


def decoded(ref, *at):
    n = ref.shape[-2] - EXTRA
    code = ref[(*at, slice(n, n + EXTRA), slice(None))].astype(jnp.int32).astype(F32)[0:1]
    steps = ref[(*at, slice(0, n), slice(None))].astype(jnp.int32).astype(F32)
    return steps * (jnp.exp2(code * (1.0 / STEPS)) * (1.0 / TOP))


def kernel(
    rows, layers, tile,
    u_hbm, v_hbm, test_hbm, ranks_hbm, offs_hbm,
    basis_ref, upd_ref,
    u_ref, v_ref, test_ref, ranks_ref, offs_ref, in_sem, unt, vt, un, um, vm, vq, uq, usel, meta, metas, probe_own, probes, parts, far_out, plain_out, chain_in, plain_in, sum_out, sum_in, core,
    mix, s_part, s_out, s_cx, s_send, s_recv, s_own, s_all, s_full, gx, linv, reach, wall, w_all, t_part, t_out, t_cx, t_send, t_recv, t_own, t_fin,
    a2v_s, a2v_r, a2u_s, a2u_r, yv_s, yv_r, yu_s, yu_r, mt_s, mt_r, pr_s, pr_r, cr_s, cr_r,
    scx_s, scx_r, srs_s, srs_r, ag_s, ag_r, agc_s, agc_r, wg_s, wg_r, tcx_s, tcx_r, trs_s, trs_r, fin_s, fin_r,
):
    ny, nz = rows // X, layers // 2
    np_, nm = nz // 2, nz - 1 - nz // 2
    br = tile // layers
    qr, hb = br // X, br // 2
    quarter = tile // X
    row, layer = lax.axis_index("row"), lax.axis_index("layer")
    x, y = lax.rem(row, X), lax.div(row, X)
    z, c = lax.div(layer, 2), lax.rem(layer, 2)

    def xdev(d):
        return (y * X + lax.rem(x + d, X), layer)

    def ydev(d):
        return (lax.rem(y + d + ny, ny) * X + x, layer)

    def zdev(d):
        return (row, lax.rem(z + d + nz, nz) * 2 + c)

    mate = (row, z * 2 + 1 - c)
    loads = [
        pltpu.make_async_copy(src, dst, in_sem.at[i])
        for i, (src, dst) in enumerate((
            (ranks_hbm, ranks_ref), (offs_hbm, offs_ref), (v_hbm, v_ref), (u_hbm, u_ref), (test_hbm, test_ref)))
    ]
    for load in loads:
        load.start()
    barrier = pltpu.get_barrier_semaphore()
    friends = [xdev(1), xdev(2), xdev(3), ydev(1), ydev(-1), zdev(1), zdev(-1), mate]
    for friend in friends:
        pl.semaphore_signal(barrier, inc=1, device_id=friend, device_id_type=pl.DeviceIdType.MESH)

    def remote(src, dst, ssem, rsem, dev):
        return pltpu.make_async_remote_copy(
            src_ref=src, dst_ref=dst, send_sem=ssem, recv_sem=rsem,
            device_id=dev, device_id_type=pl.DeviceIdType.MESH,
        )

    pending = []

    def start(copy):
        copy.start()
        pending.append(copy)
        return copy

    loads[0].wait()
    loads[1].wait()
    lanes = lax.broadcasted_iota(jnp.int32, (1, R), 1)
    live = [(lanes < ranks_ref[0, k]).astype(F32).astype(BF) for k in range(2)]

    def mask_quarter(d):
        xx = lax.rem(x + d, X)

        def body(i, carry):
            src = pl.ds(pl.multiple_of(i * br + xx * qr, qr), qr)
            dst = pl.ds(pl.multiple_of(i * qr, qr), qr)
            for k in range(2):
                v = v_ref[0, k, src, :] * live[k]
                if d == 0:
                    vq[X + x, k, dst, :] = v
                else:
                    vm[xx, k, dst, :] = v
            return carry

        lax.fori_loop(0, layers, body, 0)

    def slot_of(d):
        return lax.rem(x - d + X, X)

    def a2a(d, src, dst, ss, rs):
        return remote(src.at[lax.rem(x + d, X)], dst.at[X + x], ss.at[d], rs.at[d], xdev(d))

    def ysend(d, buf, ss, rs):
        return remote(buf.at[X + slot_of(d)], buf.at[slot_of(d)], ss.at[d], rs.at[d], ydev(1))

    yv = [ysend(d, vq, yv_s, yv_r) for d in range(X)]
    av = [None] + [a2a(d, vm, vq, a2v_s, a2v_r) for d in (1, 2, 3)]
    loads[2].wait()
    mask_quarter(0)
    pl.semaphore_wait(barrier, len(friends))
    start(yv[0])
    mask_quarter(1)
    start(av[1])
    mask_quarter(3)
    start(av[3])
    mask_quarter(2)
    for s in range(TARGETS):
        meta[s, :, :] = jnp.full((8, R), offs_ref[0, s], jnp.int32).astype(F32)
    metas[x] = meta[...]
    mts = {d: start(remote(meta, metas.at[x], mt_s.at[d], mt_r.at[d], xdev(d))) for d in (1, 2, 3)}
    loads[3].wait()
    loads[4].wait()

    def mask_left(i, carry):
        src = pl.ds(pl.multiple_of(i * br, br), br)
        for k in range(2):
            u = u_ref[0, k, src, :] * live[k]
            un[k, src, :] = u
            unt[k * R:(k + 1) * R, src] = u.T
            for xx in range(X):
                um[xx, k, pl.ds(pl.multiple_of(i * qr, qr), qr), :] = u[xx * qr:(xx + 1) * qr]
        return carry

    lax.fori_loop(0, layers, mask_left, 0)
    uq[X + x] = um[x]
    probed = dot(unt[...], test_ref[...])
    for k in range(2):
        coded(probed[k * R:(k + 1) * R], probe_own, k)
    pry = start(remote(probe_own, probes.at[FRONTS - 1], pr_s.at[0], pr_r.at[0], ydev(1)))
    for d in (1, 3):
        av[d].wait_recv()
        start(yv[d])
    start(av[2])

    def probe_send(d, src):
        return remote(src, probes.at[d - 1], pr_s.at[d], pr_r.at[d], xdev(d))

    for d in (1, 2, 3):
        @pl.when(x + d < X)
        def _(d=d):
            probe_send(d, probe_own).start()
    for k in range(2):
        vt[k, pl.ds(pl.multiple_of(x * R, R), R), :] = vq[X + x, k].T
        for d in (1, 3):
            j = slot_of(d)
            vt[k, pl.ds(pl.multiple_of(j * R, R), R), :] = vq[X + j, k].T
    pry.wait_recv()
    for d in (1, 2, 3):
        @pl.when(x + d >= X)
        def _(d=d):
            probe_send(d, probes.at[FRONTS - 1]).start()
    prx = [probe_send(d, probe_own) for d in (1, 2, 3)]
    pending.extend(prx)
    av[2].wait_recv()
    start(yv[2])
    au = {d: a2a(d, um, uq, a2u_s, a2u_r) for d in (1, 2, 3)}
    start(au[1])
    start(au[3])
    for k in range(2):
        vt[k, pl.ds(pl.multiple_of(lax.rem(x + 2, X) * R, R), R), :] = vq[X + lax.rem(x + 2, X), k].T
    for copy in mts.values():
        copy.wait_recv()

    marks = [[metas[xx, s, 0:1, :] for s in range(TARGETS)] for xx in range(X)]
    parts[...] = jnp.zeros_like(parts)

    def add_cores(slot, first, back):
        for k in range(2):
            found = dot(vt[k, first * R:, :], vq[slot, k])
            for xx in range(first, X):
                block = found[(xx - first) * R:(xx - first + 1) * R]
                for s in range(TARGETS):
                    parts[xx, s, k] += block * (marks[xx][s] == back(xx)).astype(F32)

    for j in range(X - 1):
        add_cores(X + j, j + 1, lambda xx: float(xx - j))
    yu = [ysend(d, uq, yu_s, yu_r) for d in range(X)]
    for d in (0, 1, 3, 2):
        yv[d].wait_recv()
        j = slot_of(d)
        if d == 2:
            start(yu[0])
        add_cores(j, 0, lambda xx: (X + xx - j).astype(F32))

    far = lax.rem(x + 2, X)
    right, left = lax.rem(x + 1, X), lax.rem(x + 3, X)
    def code_part(who, s):
        for k in range(2):
            coded(parts[who, s, k], far_out if who is far else plain_out, s, k)

    code_part(far, 0)
    far0 = start(remote(far_out.at[0], chain_in.at[0], cr_s.at[0], cr_r.at[0], xdev(3)))
    code_part(far, 1)
    far1 = start(remote(far_out.at[1], chain_in.at[1], cr_s.at[1], cr_r.at[1], xdev(1)))
    code_part(right, 0)
    plain0 = start(remote(plain_out.at[0], plain_in.at[0], cr_s.at[2], cr_r.at[2], xdev(1)))
    code_part(left, 1)
    plain1 = start(remote(plain_out.at[1], plain_in.at[1], cr_s.at[3], cr_r.at[3], xdev(3)))
    far0.wait_recv()
    for k in range(2):
        coded(parts[left, 0, k] + decoded(chain_in, 0, k), sum_out, 0, k)
    sum0 = start(remote(sum_out.at[0], sum_in.at[0], cr_s.at[4], cr_r.at[4], xdev(3)))
    far1.wait_recv()
    for k in range(2):
        coded(parts[right, 1, k] + decoded(chain_in, 1, k), sum_out, 1, k)
    sum1 = start(remote(sum_out.at[1], sum_in.at[1], cr_s.at[5], cr_r.at[5], xdev(1)))
    for copy in prx:
        copy.wait_recv()
    plain0.wait_recv()
    plain1.wait_recv()
    sum0.wait_recv()
    sum1.wait_recv()
    for s in range(TARGETS):
        for k in range(2):
            core[s, k] = parts[x, s, k] + decoded(plain_in, s, k) + decoded(sum_in, s, k)

    start(au[2])
    for d in (1, 3):
        au[d].wait_recv()
        start(yu[d])

    for s in range(TARGETS):
        for k in range(2):
            back = jnp.clip(offs_ref[0, s] - 1, 0, FRONTS - 1)
            mixed = dot(core[s, k], decoded(probes, back, k), precision=HIGH)
            high, low = split(mixed)
            mix[0, k * R:(k + 1) * R, s * R:(s + 1) * R] = high
            mix[1, k * R:(k + 1) * R, s * R:(s + 1) * R] = low

    def order(i):
        half = lax.div(i + 1, 2)
        off = jnp.where(lax.rem(i, 2) == 1, half - np_, np_ - half)
        return lax.rem(z + off + nz, nz)

    def pair_copy(out, cx, ss, rs, zz):
        return remote(out.at[zz], cx.at[zz], ss.at[zz], rs.at[zz], mate)

    def sketch_rows(i, carry):
        zz = order(i)
        src = pl.ds(pl.multiple_of(zz * 2 * br, 2 * br), 2 * br)
        both = jnp.concatenate([un[0, src, :], un[1, src, :]], axis=1)
        got = dot(both, mix[0]) + dot(both, mix[1])
        s_part[0, zz] = got[:br]
        s_part[1, zz] = got[br:]
        for s in range(TARGETS):
            coded(s_part[1 - c, zz, :, s * R:(s + 1) * R], s_out, zz, s)
        pair_copy(s_out, s_cx, scx_s, scx_r, zz).start()
        return carry

    chains = [(1, 0, np_), (-1, 0, nm), (1, 1, nm), (-1, 1, np_)]

    def ring_reduce(part, out, cx, send, recv, ss_cx, rs_cx, ss, rs, own, before, between):
        waited = set()

        def term(off, h):
            zz = lax.rem(z + off + 2 * nz, nz)
            if off % nz not in waited:
                waited.add(off % nz)
                pair_copy(out, cx, ss_cx, rs_cx, zz).wait_recv()
            return part[c, zz, :, h * R:(h + 1) * R] + decoded(cx, zz, h)

        def hop(ch, i):
            return remote(send.at[ch, i], recv.at[ch, i], ss.at[ch, i], rs.at[ch, i], zdev(chains[ch][0]))

        for i in range(np_):
            before(i)
            for ch, (sgn, h, n) in enumerate(chains):
                j = i - (np_ - n)
                if j < 0:
                    continue
                value = term(sgn * (n - j), h)
                if j > 0:
                    hop(ch, j - 1).wait_recv()
                    value = value + decoded(recv, ch, j - 1)
                coded(value, send, ch, j)
                start(hop(ch, j))
            between(i)
        for h in range(2):
            value = term(0, h)
            for ch, (sgn, hh, n) in enumerate(chains):
                if hh == h and n > 0:
                    hop(ch, n - 1).wait_recv()
                    value = value + decoded(recv, ch, n - 1)
            own[:, h * R:(h + 1) * R] = value

    def sketch_more(i):
        lax.fori_loop(max(2 * i - 1, 0), nz if i == np_ - 1 else 2 * i + 1, sketch_rows, 0)

    ring_reduce(
        s_part, s_out, s_cx, s_send, s_recv, scx_s, scx_r, srs_s, srs_r, s_own, sketch_more, lambda i: None)
    au[2].wait_recv()
    start(yu[2])

    for h in range(2):
        coded(s_own[:, h * R:(h + 1) * R], s_all, c, z, h)

    def gather_hop(ch, i):
        sgn, h, n = chains[ch]
        zz = lax.rem(z - sgn * i + nz, nz)
        return remote(s_all.at[c, zz, h], s_all.at[c, zz, h], ag_s.at[ch, i], ag_r.at[ch, i], zdev(sgn))

    def to_mate(off, h):
        zz = lax.rem(z + off + nz, nz)
        at = (off + nz) % nz
        return remote(s_all.at[c, zz, h], s_all.at[c, zz, h], agc_s.at[at, h], agc_r.at[at, h], mate)

    def spread(par, off, h):
        zz = lax.rem(z + off + nz, nz)
        high, low = split(decoded(s_all, par, zz, h))
        to = pl.ds(pl.multiple_of((zz * 2 + par) * br, br), br)
        s_full[0, to, h * R:(h + 1) * R] = high
        s_full[1, to, h * R:(h + 1) * R] = low

    for ch, (sgn, h, n) in enumerate(chains):
        if n > 0:
            start(gather_hop(ch, 0))
    for h in range(2):
        start(to_mate(0, h))
    pick16 = [[[(marks[xx][s] == o).astype(F32).astype(BF) for o in range(1, FRONTS + 1)]
               for s in range(TARGETS)] for xx in range(X)]

    def choose_rows(i, carry):
        src = pl.ds(pl.multiple_of(i * 32, 32), 32)
        for xx in range(X):
            for k in range(2):
                cand = [uq[X + xx - o, k, src, :] for o in range(1, FRONTS + 1)]
                for s in range(TARGETS):
                    total = cand[0] * pick16[xx][s][0]
                    for o in range(1, FRONTS):
                        total = total + cand[o] * pick16[xx][s][o]
                    usel[xx, s, src, k * R:(k + 1) * R] = total
        return carry

    for h in range(2):
        spread(c, 0, h)
    late = [(0, h) for h in range(2)]
    for i in range(np_):
        got = []
        for ch, (sgn, h, n) in enumerate(chains):
            if i < n:
                gather_hop(ch, i).wait_recv()
                if i + 1 < n:
                    start(gather_hop(ch, i + 1))
                off = -sgn * (i + 1)
                start(to_mate(off, h))
                got.append((off, h))
        for off, h in late:
            to_mate(off, h).wait_recv()
            spread(1 - c, off, h)
        for off, h in got:
            spread(c, off, h)
        if i == min(1, np_ - 1):
            for d in range(X):
                yu[d].wait_recv()
            lax.fori_loop(0, quarter // 64, choose_rows, 0)
        if i == min(2, np_ - 1):
            lax.fori_loop(quarter // 64, quarter // 32, choose_rows, 0)
        late = got
    for off, h in late:
        to_mate(off, h).wait_recv()
        spread(1 - c, off, h)

    reach[...] = jnp.zeros_like(reach)
    gx[...] = jnp.zeros_like(gx)

    def reach_rows(zz, carry):
        src = pl.ds(pl.multiple_of(zz * 2 * br, 2 * br), 2 * br)
        reach[...] += dot(unt[:, src], s_full[0, src, :]) + dot(unt[:, src], s_full[1, src, :])
        return carry

    def gram_rows(zz, carry):
        src = pl.ds(pl.multiple_of(zz * 2 * br, 2 * br), 2 * br)
        for s in range(TARGETS):
            at = slice(s * R, (s + 1) * R)
            high, low = s_full[0, src, at], s_full[1, src, at]
            gx[s] += dot(high, jnp.concatenate([high, low], axis=1), 0, 0)
        return carry

    lax.fori_loop(0, nz, reach_rows, 0)

    for s in range(TARGETS):
        for k in range(2):
            weight = dot(core[s, k], reach[k * R:(k + 1) * R, s * R:(s + 1) * R], 0, 0, precision=HIGH)
            coded(weight, w_all, x, s, k)
            high, low = split(weight)
            wall[x, s, k * R:(k + 1) * R, 0:R] = high
            wall[x, s, k * R:(k + 1) * R, R:2 * R] = low

    def weight_send(i, who, s, d):
        return remote(w_all.at[who, s], w_all.at[who, s], wg_s.at[i], wg_r.at[i], xdev(d))

    wr1 = start(weight_send(0, x, 1, 1))
    wl0 = start(weight_send(1, x, 0, 3))
    wr0 = start(weight_send(2, x, 0, 1))
    wl1 = start(weight_send(3, x, 1, 3))

    lax.fori_loop(0, nz, gram_rows, 0)
    eye = (lax.broadcasted_iota(jnp.int32, (R, R), 0) == lax.broadcasted_iota(jnp.int32, (R, R), 1)).astype(F32)
    for s in range(TARGETS):
        cross = gx[s, :, R:2 * R]
        gx[s, :, 0:R] = (gx[s, :, 0:R] + (cross + cross.T)) / tile
        gx[s, :, R:2 * R] = eye

    lane8 = lax.broadcasted_iota(jnp.int32, (8, R), 1)
    sub8 = lax.broadcasted_iota(jnp.int32, (8, R), 0)

    def factor_block(b, carry):
        r0 = pl.multiple_of(b * 8, 8)
        for s in range(TARGETS):
            gg = gx[s, pl.ds(r0, 8), 0:R]
            xx = gx[s, pl.ds(r0, 8), R:2 * R]
            cols = [
                jnp.broadcast_to(
                    jnp.sum(jnp.where(lane8 == r0 + j, gg, 0.0), axis=1, keepdims=True), (8, R))
                for j in range(8)
            ]
            diag = jnp.ones((8, R), F32)
            for j in range(8):
                pivot = cols[j][j:j + 1]
                diag = jnp.where(sub8 == j, pivot, diag)
                f = jnp.where(sub8 > j, cols[j] / pivot, 0.0)
                for m in range(j + 1, 8):
                    cols[m] = cols[m] - f * cols[m][j:j + 1]
                gg = gg - f * gg[j:j + 1]
                xx = xx - f * xx[j:j + 1]
            linv[s, pl.ds(r0, 8), :] = xx / jnp.sqrt(diag)
            lead = jnp.where(lane8 >= r0 + 8, gg / diag, 0.0)
            gx[s, :, 0:R] -= dot(lead, gg, 0, 0, precision=HIGH)
            gx[s, :, R:2 * R] -= dot(lead, xx, 0, 0, precision=HIGH)
        return carry

    blocks = R // 8
    lax.fori_loop(0, blocks // 4, factor_block, 0)
    wr1.wait_recv()
    fr1 = start(weight_send(4, left, 1, 1))
    wl0.wait_recv()
    fl0 = start(weight_send(5, right, 0, 3))

    lax.fori_loop(blocks // 4, blocks // 2, factor_block, 0)
    for copy in (wr0, wl1, fr1, fl0):
        copy.wait_recv()
    for d in (1, 2, 3):
        who = lax.rem(x + d, X)
        for s in range(TARGETS):
            for k in range(2):
                high, low = split(decoded(w_all, who, s, k))
                wall[who, s, k * R:(k + 1) * R, 0:R] = high
                wall[who, s, k * R:(k + 1) * R, R:2 * R] = low

    span = layers // 2
    for q in range(2):
        src = slice(q * span * qr, (q + 1) * span * qr)
        for xx in range(X):
            for s in range(TARGETS):
                got = dot(usel[xx, s, src, :], wall[xx, s])
                got = got[:, 0:R] + got[:, R:2 * R]
                for i in range(span):
                    t_part[i % 2, (q * span + i) // 2, xx * qr:(xx + 1) * qr, s * R:(s + 1) * R] = got[i * qr:(i + 1) * qr]
        for zz in range(q * nz // 2, (q + 1) * nz // 2):
            for s in range(TARGETS):
                coded(t_part[1 - c, zz, :, s * R:(s + 1) * R], t_out, zz, s)
            pair_copy(t_out, t_cx, tcx_s, tcx_r, zz).start()
    rest = blocks // 2

    def factor_more(i):
        lax.fori_loop(rest + i * rest // np_, rest + (i + 1) * rest // np_, factor_block, 0)

    ring_reduce(t_part, t_out, t_cx, t_send, t_recv, tcx_s, tcx_r, trs_s, trs_r, t_own, lambda i: None, factor_more)

    def final_send(d):
        at = pl.ds(pl.multiple_of(lax.rem(x + d, X) * qr, qr), qr)
        return remote(t_own.at[at, :], t_fin.at[x], fin_s.at[d], fin_r.at[d], xdev(d))

    fins = [start(final_send(d)) for d in (2, 1, 3)]
    t_fin[x] = t_own[pl.ds(pl.multiple_of(x * qr, qr), qr), :]
    for s in range(TARGETS):
        at = slice(s * R, (s + 1) * R)
        basis_ref[0, :, s, :] = dot(s_own[:, at], linv[s], 1, 1, precision=HIGH)
    for copy in fins:
        copy.wait_recv()
    for s in range(TARGETS):
        at = slice(s * R, (s + 1) * R)
        terms = jnp.concatenate([t_fin[i, :, at] for i in range(X)], axis=0)
        upd_ref[0, :, s, :] = dot(terms, linv[s], 1, 1, precision=HIGH) / tile

    for copy in pending:
        copy.wait_send()

    def pair_end(zz, carry):
        pair_copy(s_out, s_cx, scx_s, scx_r, zz).wait_send()
        pair_copy(t_out, t_cx, tcx_s, tcx_r, zz).wait_send()
        return carry

    lax.fori_loop(0, nz, pair_end, 0)


def on_device(panel_left, panel_right, test_matrix, ranks, offsets):
    rows, layers = lax.axis_size("row"), lax.axis_size("layer")
    tile = panel_left.shape[2]
    nz = layers // 2
    np_ = max(nz // 2, 1)
    br = tile // layers
    qr, hb, quarter = br // X, br // 2, tile // X
    dma = pltpu.SemaphoreType.DMA
    vmem = pltpu.VMEM
    I16 = jnp.int16
    ring = [
        vmem((2, nz, br, 2 * R), F32), vmem((nz, 2, br + EXTRA, R), I16), vmem((nz, 2, br + EXTRA, R), I16),
        vmem((4, np_, br + EXTRA, R), I16), vmem((4, np_, br + EXTRA, R), I16), vmem((br, 2 * R), F32),
    ]
    scratch = [
        vmem((1, 2, tile, R), BF), vmem((1, 2, tile, R), BF), vmem((tile, R), BF),
        pltpu.SMEM((1, 2), jnp.int32), pltpu.SMEM((1, TARGETS), jnp.int32), dma((5,)),
        vmem((2 * R, tile), BF), vmem((2, X * R, quarter), BF),
        vmem((2, tile, R), BF), vmem((X, 2, quarter, R), BF), vmem((X, 2, quarter, R), BF),
        vmem((2 * X, 2, quarter, R), BF), vmem((2 * X, 2, quarter, R), BF),
        vmem((X, TARGETS, quarter, 2 * R), BF),
        vmem((TARGETS, 8, R), F32), vmem((X, TARGETS, 8, R), F32),
        vmem((2, R + EXTRA, R), I16), vmem((FRONTS, 2, R + EXTRA, R), I16),
        vmem((X, TARGETS, 2, R, R), F32),
        *[vmem((TARGETS, 2, R + EXTRA, R), I16)] * 6,
        vmem((TARGETS, 2, R, R), F32),
        vmem((2, 2 * R, 2 * R), BF),
        *ring,
        vmem((2, nz, 2, br + EXTRA, R), I16), vmem((2, tile, 2 * R), BF),
        vmem((TARGETS, R, 2 * R), F32), vmem((TARGETS, R, R), F32), vmem((2 * R, 2 * R), F32),
        vmem((X, TARGETS, 2 * R, 2 * R), BF), vmem((X, TARGETS, 2, R + EXTRA, R), I16),
        *ring,
        vmem((X, qr, 2 * R), F32),
        dma((X,)), dma((X,)), dma((X,)), dma((X,)), dma((X,)), dma((X,)), dma((X,)), dma((X,)),
        dma((X,)), dma((X,)), dma((X,)), dma((X,)), dma((6,)), dma((6,)),
        dma((nz,)), dma((nz,)), dma((4, np_)), dma((4, np_)),
        dma((4, np_)), dma((4, np_)), dma((nz, 2)), dma((nz, 2)),
        dma((6,)), dma((6,)),
        dma((nz,)), dma((nz,)), dma((4, np_)), dma((4, np_)),
        dma((X,)), dma((X,)),
    ]
    inside = pl.BlockSpec(memory_space=pltpu.VMEM)
    outside = pl.BlockSpec(memory_space=pltpu.HBM)
    out = jax.ShapeDtypeStruct((1, br, TARGETS, R), F32)
    return pl.pallas_call(
        functools.partial(kernel, rows, layers, tile),
        out_shape=(out, out),
        in_specs=[outside] * 5,
        out_specs=(inside, inside),
        scratch_shapes=scratch,
        compiler_params=pltpu.CompilerParams(
            collective_id=0, has_side_effects=True, vmem_limit_bytes=64 * 2**20
        ),
        name="trailing_update",
    )(panel_left, panel_right, test_matrix, ranks, offsets)


def solution(mesh):
    return jax.shard_map(
        on_device,
        mesh=mesh,
        in_specs=(
            P("row", "layer", None, None),
            P("row", "layer", None, None),
            P(),
            P("row", "layer"),
            P("row", None),
        ),
        out_specs=(P("row", "layer", None, None), P("row", "layer", None, None)),
        check_vma=False,
    )
```

time: 146 us -> 120 us (0.82)
  Pallas kernels: 138 us -> 116 us
  local copies, waits for them, and re-layouts: 6.11 us -> 2.26 us
    pallas_call x1, Pallas kernels: 138 us -> 116 us  [on_device(): pl.pallas_call(functools.partial(kernel, rows, layers, tile), out_shape=(...]
    unnamed x12 -> x4, local copies, waits for them, and re-layouts: 6.11 us -> 2.26 us
where the time goes in v2:
time: 120 us; the launch traced here: 119 us
  Pallas kernels  116 us (97%)
  local copies, waits for them, and re-layouts  2.26 us (2%)
    pallas_call x1, Pallas kernels, on_device(): pl.pallas_call(functools.partial(kernel, rows, layers, tile), out_shape=(...  116 us

profile of v2, /device:TPU:6, one launch (start us, length us, event | category | flops | bytes accessed | tf_op | source)
XLA Modules:
  0.0 119.1 jit_solution(6040254876356029353)
XLA Ops:
  0.6 116.2 %trailing_update.1 = (f32[1,128,2,128]{3,2,1,0:T(2,128)}, f32[1,128,2,128]{3,2,1,0:T(2,128)}) custom-call(bf16[1,2,2048,128]{3,2,1,0:T(8,128)(2,1)} %u_hbm.1, bf16[1,2,2048,128]{3,2,1,0:T(8,128)(2,1)} %v_hbm.1, bf16[2048,128]{1,0:T(8,128)(2,1)} %test_hbm.1, s32[1,2]{1,0:T(1,128)} %ranks_hbm.1, s32[1,2]{1,0:T(1,128)} %offs_hbm.1), custom_call_target="tpu_custom_call" | custom-call | tf_op jit(solution)/shard_map/trailing_update/pallas_call | solution.py:582
  116.9 0.0 copy-start
  116.9 1.6 %copy.9 = f32[1,128,2,128]{3,2,1,0:T(2,128)} copy(f32[1,128,2,128]{3,2,1,0:T(2,128)} %get-tuple-element.4) | data formatting | bytes 262144
  118.5 0.0 copy-done
  118.5 0.7 copy.10
Async XLA Ops:
  116.9 1.6 %copy-start = (f32[1,128,2,128]{3,2,1,0:T(2,128)S(1)}, f32[1,128,2,128]{3,2,1,0:T(2,128)}, u32[]{:S(2)}) copy-start(f32[1,128,2,128]{3,2,1,0:T(2,128)} %get-tuple-element.5) | copy-start | bytes 393220

commit v3 on v2

--- a/solution.py
+++ b/solution.py
@@ -87,7 +87,12 @@
     for load in loads:
         load.start()
     barrier = pltpu.get_barrier_semaphore()
-    friends = [xdev(1), xdev(2), xdev(3), ydev(1), ydev(-1), zdev(1), zdev(-1), mate]
+
+    def zcross(d):
+        return (row, lax.rem(z + d + nz, nz) * 2 + 1 - c)
+
+    friends = [
+        xdev(1), xdev(2), xdev(3), ydev(1), ydev(-1), zdev(1), zdev(-1), zcross(1), zcross(-1), mate]
     for friend in friends:
         pl.semaphore_signal(barrier, inc=1, device_id=friend, device_id_type=pl.DeviceIdType.MESH)
 
@@ -289,6 +294,7 @@
         return carry
 
     chains = [(1, 0, np_), (-1, 0, nm), (1, 1, nm), (-1, 1, np_)]
+    groups = ((0, 3), (1, 2))
 
     def ring_reduce(part, out, cx, send, recv, ss_cx, rs_cx, ss, rs, own, before, between):
         waited = set()
@@ -303,19 +309,24 @@
         def hop(ch, i):
             return remote(send.at[ch, i], recv.at[ch, i], ss.at[ch, i], rs.at[ch, i], zdev(chains[ch][0]))
 
+        before(0)
         for i in range(np_):
-            before(i)
-            for ch, (sgn, h, n) in enumerate(chains):
-                j = i - (np_ - n)
-                if j < 0:
-                    continue
-                value = term(sgn * (n - j), h)
-                if j > 0:
-                    hop(ch, j - 1).wait_recv()
-                    value = value + decoded(recv, ch, j - 1)
-                coded(value, send, ch, j)
-                start(hop(ch, j))
-            between(i)
+            for group in groups:
+                if i == 0 and group is groups[1] and np_ > 1:
+                    before(1)
+                for ch in group:
+                    sgn, h, n = chains[ch]
+                    if i >= n:
+                        continue
+                    value = term(sgn * (n - i), h)
+                    if i > 0:
+                        hop(ch, i - 1).wait_recv()
+                        value = value + decoded(recv, ch, i - 1)
+                    coded(value, send, ch, i)
+                    start(hop(ch, i))
+                between()
+            if i + 2 < np_:
+                before(i + 2)
         for h in range(2):
             value = term(0, h)
             for ch, (sgn, hh, n) in enumerate(chains):
@@ -328,7 +339,7 @@
         lax.fori_loop(max(2 * i - 1, 0), nz if i == np_ - 1 else 2 * i + 1, sketch_rows, 0)
 
     ring_reduce(
-        s_part, s_out, s_cx, s_send, s_recv, scx_s, scx_r, srs_s, srs_r, s_own, sketch_more, lambda i: None)
+        s_part, s_out, s_cx, s_send, s_recv, scx_s, scx_r, srs_s, srs_r, s_own, sketch_more, lambda: None)
     au[2].wait_recv()
     start(yu[2])
 
@@ -352,11 +363,65 @@
         s_full[0, to, h * R:(h + 1) * R] = high
         s_full[1, to, h * R:(h + 1) * R] = low
 
-    for ch, (sgn, h, n) in enumerate(chains):
-        if n > 0:
-            start(gather_hop(ch, 0))
+    def launch(ch, i):
+        sgn, h, n = chains[ch]
+        start(gather_hop(ch, i))
+        if n == np_ and i == n - 1:
+            zz = lax.rem(z - sgn * i + nz, nz)
+            at = (-sgn * n) % nz
+            start(remote(s_all.at[c, zz, h], s_all.at[c, zz, h], agc_s.at[at, h], agc_r.at[at, h], zcross(sgn)))
+
+    def use(off):
+        zz = lax.rem(z + off + nz, nz)
+        src = pl.ds(pl.multiple_of(zz * 2 * br, 2 * br), 2 * br)
+        reach[...] += dot(unt[:, src], s_full[0, src, :]) + dot(unt[:, src], s_full[1, src, :])
+        for s in range(TARGETS):
+            at = slice(s * R, (s + 1) * R)
+            high, low = s_full[0, src, at], s_full[1, src, at]
+            gx[s] += dot(high, jnp.concatenate([high, low], axis=1), 0, 0)
+
+    for ch in groups[0]:
+        launch(ch, 0)
+    reach[...] = jnp.zeros_like(reach)
+    gx[...] = jnp.zeros_like(gx)
+    for h in range(2):
+        spread(c, 0, h)
+    for ch in groups[1]:
+        if chains[ch][2] > 0:
+            launch(ch, 0)
     for h in range(2):
         start(to_mate(0, h))
+    late = [(0, h) for h in range(2)]
+    for i in range(np_):
+        got = []
+        ready = sorted({i, -i})
+        for group in groups:
+            for ch in group:
+                sgn, h, n = chains[ch]
+                if i < n:
+                    gather_hop(ch, i).wait_recv()
+                    if i + 1 < n:
+                        launch(ch, i + 1)
+                    off = -sgn * (i + 1)
+                    if i < np_ - 1:
+                        start(to_mate(off, h))
+                    got.append((off, h))
+            if group is groups[0]:
+                for off, h in late:
+                    to_mate(off, h).wait_recv()
+                    spread(1 - c, off, h)
+                use(ready[0])
+            else:
+                for off, h in got:
+                    spread(c, off, h)
+                for off in ready[1:]:
+                    use(off)
+        late = got
+    for off, h in late:
+        to_mate(off, h).wait_recv()
+        spread(1 - c, off, h)
+    use(np_)
+
     pick16 = [[[(marks[xx][s] == o).astype(F32).astype(BF) for o in range(1, FRONTS + 1)]
                for s in range(TARGETS)] for xx in range(X)]
 
@@ -372,53 +437,6 @@
                     usel[xx, s, src, k * R:(k + 1) * R] = total
         return carry
 
-    for h in range(2):
-        spread(c, 0, h)
-    late = [(0, h) for h in range(2)]
-    for i in range(np_):
-        got = []
-        for ch, (sgn, h, n) in enumerate(chains):
-            if i < n:
-                gather_hop(ch, i).wait_recv()
-                if i + 1 < n:
-                    start(gather_hop(ch, i + 1))
-                off = -sgn * (i + 1)
-                start(to_mate(off, h))
-                got.append((off, h))
-        for off, h in late:
-            to_mate(off, h).wait_recv()
-            spread(1 - c, off, h)
-        for off, h in got:
-            spread(c, off, h)
-        if i == min(1, np_ - 1):
-            for d in range(X):
-                yu[d].wait_recv()
-            lax.fori_loop(0, quarter // 64, choose_rows, 0)
-        if i == min(2, np_ - 1):
-            lax.fori_loop(quarter // 64, quarter // 32, choose_rows, 0)
-        late = got
-    for off, h in late:
-        to_mate(off, h).wait_recv()
-        spread(1 - c, off, h)
-
-    reach[...] = jnp.zeros_like(reach)
-    gx[...] = jnp.zeros_like(gx)
-
-    def reach_rows(zz, carry):
-        src = pl.ds(pl.multiple_of(zz * 2 * br, 2 * br), 2 * br)
-        reach[...] += dot(unt[:, src], s_full[0, src, :]) + dot(unt[:, src], s_full[1, src, :])
-        return carry
-
-    def gram_rows(zz, carry):
-        src = pl.ds(pl.multiple_of(zz * 2 * br, 2 * br), 2 * br)
-        for s in range(TARGETS):
-            at = slice(s * R, (s + 1) * R)
-            high, low = s_full[0, src, at], s_full[1, src, at]
-            gx[s] += dot(high, jnp.concatenate([high, low], axis=1), 0, 0)
-        return carry
-
-    lax.fori_loop(0, nz, reach_rows, 0)
-
     for s in range(TARGETS):
         for k in range(2):
             weight = dot(core[s, k], reach[k * R:(k + 1) * R, s * R:(s + 1) * R], 0, 0, precision=HIGH)
@@ -435,7 +453,6 @@
     wr0 = start(weight_send(2, x, 0, 1))
     wl1 = start(weight_send(3, x, 1, 3))
 
-    lax.fori_loop(0, nz, gram_rows, 0)
     eye = (lax.broadcasted_iota(jnp.int32, (R, R), 0) == lax.broadcasted_iota(jnp.int32, (R, R), 1)).astype(F32)
     for s in range(TARGETS):
         cross = gx[s, :, R:2 * R]
@@ -466,8 +483,7 @@
                 xx = xx - f * xx[j:j + 1]
             linv[s, pl.ds(r0, 8), :] = xx / jnp.sqrt(diag)
             lead = jnp.where(lane8 >= r0 + 8, gg / diag, 0.0)
-            gx[s, :, 0:R] -= dot(lead, gg, 0, 0, precision=HIGH)
-            gx[s, :, R:2 * R] -= dot(lead, xx, 0, 0, precision=HIGH)
+            gx[s] -= dot(lead, jnp.concatenate([gg, xx], axis=1), 0, 0, precision=HIGH)
         return carry
 
     blocks = R // 8
@@ -477,7 +493,9 @@
     wl0.wait_recv()
     fl0 = start(weight_send(5, right, 0, 3))
 
-    lax.fori_loop(blocks // 4, blocks // 2, factor_block, 0)
+    for d in range(X):
+        yu[d].wait_recv()
+    lax.fori_loop(0, quarter // 32, choose_rows, 0)
     for copy in (wr0, wl1, fr1, fl0):
         copy.wait_recv()
     for d in (1, 2, 3):
@@ -501,11 +519,14 @@
             for s in range(TARGETS):
                 coded(t_part[1 - c, zz, :, s * R:(s + 1) * R], t_out, zz, s)
             pair_copy(t_out, t_cx, tcx_s, tcx_r, zz).start()
-    rest = blocks // 2
-
-    def factor_more(i):
-        lax.fori_loop(rest + i * rest // np_, rest + (i + 1) * rest // np_, factor_block, 0)
-
+    factored = [blocks // 4]
+
+    def factor_more(count=1):
+        upto = min(factored[0] + count, blocks)
+        lax.fori_loop(factored[0], upto, factor_block, 0)
+        factored[0] = upto
+
+    factor_more(2)
     ring_reduce(t_part, t_out, t_cx, t_send, t_recv, tcx_s, tcx_r, trs_s, trs_r, t_own, lambda i: None, factor_more)
 
     def final_send(d):
@@ -514,6 +535,7 @@
 
     fins = [start(final_send(d)) for d in (2, 1, 3)]
     t_fin[x] = t_own[pl.ds(pl.multiple_of(x * qr, qr), qr), :]
+    factor_more(blocks)
     for s in range(TARGETS):
         at = slice(s * R, (s + 1) * R)
         basis_ref[0, :, s, :] = dot(s_own[:, at], linv[s], 1, 1, precision=HIGH)

time: 120 us -> 116 us (0.967)
  Pallas kernels: 116 us -> 113 us
    pallas_call x1, Pallas kernels: 116 us -> 113 us  [on_device(): pl.pallas_call(functools.partial(kernel, rows, layers, tile), out_shape=(...]
where the time goes in v3:
time: 116 us
  Pallas kernels  113 us (97%)
  local copies, waits for them, and re-layouts  2.26 us (2%)
    pallas_call x1, Pallas kernels, on_device(): pl.pallas_call(functools.partial(kernel, rows, layers, tile), out_shape=(...  113 us

profile of v3, /device:TPU:6, one launch (start us, length us, event | category | flops | bytes accessed | tf_op | source)
XLA Modules:
  0.0 115.7 jit_solution(9999725002861074967)
XLA Ops:
  0.6 112.7 %trailing_update.1 = (f32[1,128,2,128]{3,2,1,0:T(2,128)}, f32[1,128,2,128]{3,2,1,0:T(2,128)}) custom-call(bf16[1,2,2048,128]{3,2,1,0:T(8,128)(2,1)} %u_hbm.1, bf16[1,2,2048,128]{3,2,1,0:T(8,128)(2,1)} %v_hbm.1, bf16[2048,128]{1,0:T(8,128)(2,1)} %test_hbm.1, s32[1,2]{1,0:T(1,128)} %ranks_hbm.1, s32[1,2]{1,0:T(1,128)} %offs_hbm.1), custom_call_target="tpu_custom_call" | custom-call | tf_op jit(solution)/shard_map/trailing_update/pallas_call | solution.py:604
  113.4 0.0 copy-start
  113.4 1.6 %copy.9 = f32[1,128,2,128]{3,2,1,0:T(2,128)} copy(f32[1,128,2,128]{3,2,1,0:T(2,128)} %get-tuple-element.4) | data formatting | bytes 262144
  115.0 0.0 copy-done
  115.0 0.7 copy.10
Async XLA Ops:
  113.4 1.6 %copy-start = (f32[1,128,2,128]{3,2,1,0:T(2,128)S(1)}, f32[1,128,2,128]{3,2,1,0:T(2,128)}, u32[]{:S(2)}) copy-start(f32[1,128,2,128]{3,2,1,0:T(2,128)} %get-tuple-element.5) | copy-start | bytes 393220

commit v4 on v3

--- a/solution.py
+++ b/solution.py
@@ -139,16 +139,27 @@
     def ysend(d, buf, ss, rs):
         return remote(buf.at[X + slot_of(d)], buf.at[slot_of(d)], ss.at[d], rs.at[d], ydev(1))
 
-    yv = [ysend(d, vq, yv_s, yv_r) for d in range(X)]
-    av = [None] + [a2a(d, vm, vq, a2v_s, a2v_r) for d in (1, 2, 3)]
+    yv = {
+        (d, k): remote(
+            vq.at[X + slot_of(d), k], vq.at[slot_of(d), k], yv_s.at[d, k], yv_r.at[d, k], ydev(1))
+        for d in range(X) for k in range(2)
+    }
+    av = {
+        (d, k): remote(
+            vm.at[lax.rem(x + d, X), k], vq.at[X + x, k], a2v_s.at[d, k], a2v_r.at[d, k], xdev(d))
+        for d in (1, 2, 3) for k in range(2)
+    }
     loads[2].wait()
     mask_quarter(0)
     pl.semaphore_wait(barrier, len(friends))
-    start(yv[0])
+    start(yv[0, 0])
+    start(yv[0, 1])
     mask_quarter(1)
-    start(av[1])
+    start(av[1, 0])
     mask_quarter(3)
-    start(av[3])
+    start(av[3, 0])
+    start(av[1, 1])
+    start(av[3, 1])
     mask_quarter(2)
     for s in range(TARGETS):
         meta[s, :, :] = jnp.full((8, R), offs_ref[0, s], jnp.int32).astype(F32)
@@ -174,9 +185,9 @@
         coded(probed[k * R:(k + 1) * R], probe_own, k)
     pry = start(remote(probe_own, probes.at[FRONTS - 1], pr_s.at[0], pr_r.at[0], ydev(1)))
     for d in (1, 3):
-        av[d].wait_recv()
-        start(yv[d])
-    start(av[2])
+        av[d, 0].wait_recv()
+        start(yv[d, 0])
+    start(av[2, 0])
 
     def probe_send(d, src):
         return remote(src, probes.at[d - 1], pr_s.at[d], pr_r.at[d], xdev(d))
@@ -185,11 +196,18 @@
         @pl.when(x + d < X)
         def _(d=d):
             probe_send(d, probe_own).start()
-    for k in range(2):
-        vt[k, pl.ds(pl.multiple_of(x * R, R), R), :] = vq[X + x, k].T
-        for d in (1, 3):
-            j = slot_of(d)
-            vt[k, pl.ds(pl.multiple_of(j * R, R), R), :] = vq[X + j, k].T
+    def turn(d, k):
+        j = slot_of(d)
+        vt[k, pl.ds(pl.multiple_of(j * R, R), R), :] = vq[X + j, k].T
+
+    turn(0, 0)
+    turn(0, 1)
+    turn(1, 0)
+    turn(3, 0)
+    av[2, 0].wait_recv()
+    start(yv[2, 0])
+    start(av[2, 1])
+    turn(2, 0)
     pry.wait_recv()
     for d in (1, 2, 3):
         @pl.when(x + d >= X)
@@ -197,81 +215,93 @@
             probe_send(d, probes.at[FRONTS - 1]).start()
     prx = [probe_send(d, probe_own) for d in (1, 2, 3)]
     pending.extend(prx)
-    av[2].wait_recv()
-    start(yv[2])
     au = {d: a2a(d, um, uq, a2u_s, a2u_r) for d in (1, 2, 3)}
-    start(au[1])
-    start(au[3])
-    for k in range(2):
-        vt[k, pl.ds(pl.multiple_of(lax.rem(x + 2, X) * R, R), R), :] = vq[X + lax.rem(x + 2, X), k].T
     for copy in mts.values():
         copy.wait_recv()
 
     marks = [[metas[xx, s, 0:1, :] for s in range(TARGETS)] for xx in range(X)]
     parts[...] = jnp.zeros_like(parts)
 
-    def add_cores(slot, first, back):
-        for k in range(2):
-            found = dot(vt[k, first * R:, :], vq[slot, k])
-            for xx in range(first, X):
-                block = found[(xx - first) * R:(xx - first + 1) * R]
-                for s in range(TARGETS):
-                    parts[xx, s, k] += block * (marks[xx][s] == back(xx)).astype(F32)
-
-    for j in range(X - 1):
-        add_cores(X + j, j + 1, lambda xx: float(xx - j))
-    yu = [ysend(d, uq, yu_s, yu_r) for d in range(X)]
-    for d in (0, 1, 3, 2):
-        yv[d].wait_recv()
+    def add_cores(k, slot, first, back):
+        found = dot(vt[k, first * R:, :], vq[slot, k])
+        for xx in range(first, X):
+            block = found[(xx - first) * R:(xx - first + 1) * R]
+            for s in range(TARGETS):
+                parts[xx, s, k] += block * (marks[xx][s] == back(xx)).astype(F32)
+
+    def add_same(k):
+        for j in range(X - 1):
+            add_cores(k, X + j, j + 1, lambda xx: float(xx - j))
+
+    def add_arrived(d, k):
+        yv[d, k].wait_recv()
         j = slot_of(d)
-        if d == 2:
-            start(yu[0])
-        add_cores(j, 0, lambda xx: (X + xx - j).astype(F32))
+        add_cores(k, j, 0, lambda xx: (X + xx - j).astype(F32))
 
     far = lax.rem(x + 2, X)
     right, left = lax.rem(x + 1, X), lax.rem(x + 3, X)
-    def code_part(who, s):
-        for k in range(2):
-            coded(parts[who, s, k], far_out if who is far else plain_out, s, k)
-
-    code_part(far, 0)
-    far0 = start(remote(far_out.at[0], chain_in.at[0], cr_s.at[0], cr_r.at[0], xdev(3)))
-    code_part(far, 1)
-    far1 = start(remote(far_out.at[1], chain_in.at[1], cr_s.at[1], cr_r.at[1], xdev(1)))
-    code_part(right, 0)
-    plain0 = start(remote(plain_out.at[0], plain_in.at[0], cr_s.at[2], cr_r.at[2], xdev(1)))
-    code_part(left, 1)
-    plain1 = start(remote(plain_out.at[1], plain_in.at[1], cr_s.at[3], cr_r.at[3], xdev(3)))
-    far0.wait_recv()
-    for k in range(2):
-        coded(parts[left, 0, k] + decoded(chain_in, 0, k), sum_out, 0, k)
-    sum0 = start(remote(sum_out.at[0], sum_in.at[0], cr_s.at[4], cr_r.at[4], xdev(3)))
-    far1.wait_recv()
-    for k in range(2):
-        coded(parts[right, 1, k] + decoded(chain_in, 1, k), sum_out, 1, k)
-    sum1 = start(remote(sum_out.at[1], sum_in.at[1], cr_s.at[5], cr_r.at[5], xdev(1)))
-    for copy in prx:
-        copy.wait_recv()
-    plain0.wait_recv()
-    plain1.wait_recv()
-    sum0.wait_recv()
-    sum1.wait_recv()
-    for s in range(TARGETS):
-        for k in range(2):
-            core[s, k] = parts[x, s, k] + decoded(plain_in, s, k) + decoded(sum_in, s, k)
-
-    start(au[2])
-    for d in (1, 3):
-        au[d].wait_recv()
-        start(yu[d])
-
-    for s in range(TARGETS):
-        for k in range(2):
+
+    def core_hop(i, k, out, into, s, d):
+        return remote(out.at[s, k], into.at[s, k], cr_s.at[i, k], cr_r.at[i, k], xdev(d))
+
+    trips = [(far, far_out, chain_in, s, 2) for s in range(2)]
+    trips += [(right, plain_out, plain_in, s, 1) for s in range(2)] + [(left, sum_out, sum_in, s, 3) for s in range(2)]
+
+    def cores_out(k):
+        for i, (who, out, into, s, d) in enumerate(trips):
+            coded(parts[who, s, k], out, s, k)
+            start(core_hop(i, k, out, into, s, d))
+
+    def cores_in(k):
+        for i, (who, out, into, s, d) in enumerate(trips):
+            core_hop(i, k, out, into, s, d).wait_recv()
+        for s in range(TARGETS):
+            core[s, k] = (
+                parts[x, s, k] + decoded(chain_in, s, k) + decoded(plain_in, s, k) + decoded(sum_in, s, k))
+
+    def mix_layer(k):
+        for s in range(TARGETS):
             back = jnp.clip(offs_ref[0, s] - 1, 0, FRONTS - 1)
             mixed = dot(core[s, k], decoded(probes, back, k), precision=HIGH)
             high, low = split(mixed)
             mix[0, k * R:(k + 1) * R, s * R:(s + 1) * R] = high
             mix[1, k * R:(k + 1) * R, s * R:(s + 1) * R] = low
+
+    yu = [ysend(d, uq, yu_s, yu_r) for d in range(X)]
+    add_same(0)
+    for d in (0, 1, 3):
+        add_arrived(d, 0)
+    av[1, 1].wait_recv()
+    start(yv[1, 1])
+    av[3, 1].wait_recv()
+    turn(1, 1)
+    turn(3, 1)
+    yv[2, 0].wait_recv()
+    start(yv[3, 1])
+    av[2, 1].wait_recv()
+    start(yv[2, 1])
+    last = slot_of(2)
+    add_cores(0, last, 0, lambda xx: (X + xx - last).astype(F32))
+    cores_out(0)
+    turn(2, 1)
+    add_same(1)
+    start(au[1])
+    start(au[3])
+    add_arrived(0, 1)
+    add_arrived(1, 1)
+    for copy in prx:
+        copy.wait_recv()
+    cores_in(0)
+    mix_layer(0)
+    add_arrived(3, 1)
+    yv[2, 1].wait_recv()
+    start(yu[0])
+    add_cores(1, last, 0, lambda xx: (X + xx - last).astype(F32))
+    cores_out(1)
+    cores_in(1)
+
+    start(au[2])
+    mix_layer(1)
 
     def order(i):
         half = lax.div(i + 1, 2)
@@ -337,6 +367,10 @@
 
     def sketch_more(i):
         lax.fori_loop(max(2 * i - 1, 0), nz if i == np_ - 1 else 2 * i + 1, sketch_rows, 0)
+        if i == min(1, np_ - 1):
+            for d in (1, 3):
+                au[d].wait_recv()
+                start(yu[d])
 
     ring_reduce(
         s_part, s_out, s_cx, s_send, s_recv, scx_s, scx_r, srs_s, srs_r, s_own, sketch_more, lambda: None)
@@ -590,8 +624,8 @@
         vmem((X, TARGETS, 2 * R, 2 * R), BF), vmem((X, TARGETS, 2, R + EXTRA, R), I16),
         *ring,
         vmem((X, qr, 2 * R), F32),
-        dma((X,)), dma((X,)), dma((X,)), dma((X,)), dma((X,)), dma((X,)), dma((X,)), dma((X,)),
-        dma((X,)), dma((X,)), dma((X,)), dma((X,)), dma((6,)), dma((6,)),
+        dma((X, 2)), dma((X, 2)), dma((X,)), dma((X,)), dma((X, 2)), dma((X, 2)), dma((X,)), dma((X,)),
+        dma((X,)), dma((X,)), dma((X,)), dma((X,)), dma((6, 2)), dma((6, 2)),
         dma((nz,)), dma((nz,)), dma((4, np_)), dma((4, np_)),
         dma((4, np_)), dma((4, np_)), dma((nz, 2)), dma((nz, 2)),
         dma((6,)), dma((6,)),

time: 116 us -> 110 us (0.948)
  Pallas kernels: 113 us -> 106 us
    pallas_call x1, Pallas kernels: 113 us -> 106 us  [on_device(): pl.pallas_call(functools.partial(kernel, rows, layers, tile), out_shape=(...]
where the time goes in v4:
time: 110 us; the launch traced here: 109 us
  Pallas kernels  106 us (96%)
  local copies, waits for them, and re-layouts  2.26 us (2%)
    pallas_call x1, Pallas kernels, on_device(): pl.pallas_call(functools.partial(kernel, rows, layers, tile), out_shape=(...  106 us
    unnamed x4, local copies, waits for them, and re-layouts  2.26 us

profile of v4, /device:TPU:6, one launch (start us, length us, event | category | flops | bytes accessed | tf_op | source)
XLA Modules:
  0.0 109.4 jit_solution(4573614439387005343)
XLA Ops:
  0.6 106.5 %trailing_update.1 = (f32[1,128,2,128]{3,2,1,0:T(2,128)}, f32[1,128,2,128]{3,2,1,0:T(2,128)}) custom-call(bf16[1,2,2048,128]{3,2,1,0:T(8,128)(2,1)} %u_hbm.1, bf16[1,2,2048,128]{3,2,1,0:T(8,128)(2,1)} %v_hbm.1, bf16[2048,128]{1,0:T(8,128)(2,1)} %test_hbm.1, s32[1,2]{1,0:T(1,128)} %ranks_hbm.1, s32[1,2]{1,0:T(1,128)} %offs_hbm.1), custom_call_target="tpu_custom_call" | custom-call | tf_op jit(solution)/shard_map/trailing_update/pallas_call | solution.py:638
  107.1 0.0 copy-start
  107.1 1.6 %copy.9 = f32[1,128,2,128]{3,2,1,0:T(2,128)} copy(f32[1,128,2,128]{3,2,1,0:T(2,128)} %get-tuple-element.4) | data formatting | bytes 262144
  108.7 0.0 copy-done
  108.7 0.7 copy.10
Async XLA Ops:
  107.1 1.6 %copy-start = (f32[1,128,2,128]{3,2,1,0:T(2,128)S(1)}, f32[1,128,2,128]{3,2,1,0:T(2,128)}, u32[]{:S(2)}) copy-start(f32[1,128,2,128]{3,2,1,0:T(2,128)} %get-tuple-element.5) | copy-start | bytes 393220

commit v5 on v4

--- a/solution.py
+++ b/solution.py
@@ -92,7 +92,8 @@
         return (row, lax.rem(z + d + nz, nz) * 2 + 1 - c)
 
     friends = [
-        xdev(1), xdev(2), xdev(3), ydev(1), ydev(-1), zdev(1), zdev(-1), zcross(1), zcross(-1), mate]
+        xdev(1), xdev(2), xdev(3), ydev(1), ydev(-1), zdev(1), zdev(-1), zcross(1), zcross(-1), mate,
+        zdev(2), zdev(-2), zcross(2), zcross(-2)]
     for friend in friends:
         pl.semaphore_signal(barrier, inc=1, device_id=friend, device_id_type=pl.DeviceIdType.MESH)
 
@@ -380,10 +381,15 @@
     for h in range(2):
         coded(s_own[:, h * R:(h + 1) * R], s_all, c, z, h)
 
+    def gather_leg(ch, i):
+        sgn = chains[ch][0]
+        return (0, sgn * (i + 1)) if i < 2 else (-2 * sgn, sgn * (i - 1))
+
     def gather_hop(ch, i):
-        sgn, h, n = chains[ch]
-        zz = lax.rem(z - sgn * i + nz, nz)
-        return remote(s_all.at[c, zz, h], s_all.at[c, zz, h], ag_s.at[ch, i], ag_r.at[ch, i], zdev(sgn))
+        h = chains[ch][1]
+        off, d = gather_leg(ch, i)
+        zz = lax.rem(z + off + nz, nz)
+        return remote(s_all.at[c, zz, h], s_all.at[c, zz, h], ag_s.at[ch, i], ag_r.at[ch, i], zdev(d))
 
     def to_mate(off, h):
         zz = lax.rem(z + off + nz, nz)
@@ -401,9 +407,10 @@
         sgn, h, n = chains[ch]
         start(gather_hop(ch, i))
         if n == np_ and i == n - 1:
-            zz = lax.rem(z - sgn * i + nz, nz)
+            off, d = gather_leg(ch, i)
+            zz = lax.rem(z + off + nz, nz)
             at = (-sgn * n) % nz
-            start(remote(s_all.at[c, zz, h], s_all.at[c, zz, h], agc_s.at[at, h], agc_r.at[at, h], zcross(sgn)))
+            start(remote(s_all.at[c, zz, h], s_all.at[c, zz, h], agc_s.at[at, h], agc_r.at[at, h], zcross(d)))
 
     def use(off):
         zz = lax.rem(z + off + nz, nz)
@@ -415,14 +422,15 @@
             gx[s] += dot(high, jnp.concatenate([high, low], axis=1), 0, 0)
 
     for ch in groups[0]:
-        launch(ch, 0)
+        for i in range(min(2, chains[ch][2])):
+            launch(ch, i)
     reach[...] = jnp.zeros_like(reach)
     gx[...] = jnp.zeros_like(gx)
     for h in range(2):
         spread(c, 0, h)
     for ch in groups[1]:
-        if chains[ch][2] > 0:
-            launch(ch, 0)
+        for i in range(min(2, chains[ch][2])):
+            launch(ch, i)
     for h in range(2):
         start(to_mate(0, h))
     late = [(0, h) for h in range(2)]
@@ -434,8 +442,8 @@
                 sgn, h, n = chains[ch]
                 if i < n:
                     gather_hop(ch, i).wait_recv()
-                    if i + 1 < n:
-                        launch(ch, i + 1)
+                    for j in range(2, n if i == 1 else 2):
+                        launch(ch, j)
                     off = -sgn * (i + 1)
                     if i < np_ - 1:
                         start(to_mate(off, h))
@@ -482,10 +490,7 @@
     def weight_send(i, who, s, d):
         return remote(w_all.at[who, s], w_all.at[who, s], wg_s.at[i], wg_r.at[i], xdev(d))
 
-    wr1 = start(weight_send(0, x, 1, 1))
-    wl0 = start(weight_send(1, x, 0, 3))
-    wr0 = start(weight_send(2, x, 0, 1))
-    wl1 = start(weight_send(3, x, 1, 3))
+    shares = [start(weight_send(i, x, i % 2, d)) for i, d in enumerate((2, 2, 1, 1, 3, 3))]
 
     eye = (lax.broadcasted_iota(jnp.int32, (R, R), 0) == lax.broadcasted_iota(jnp.int32, (R, R), 1)).astype(F32)
     for s in range(TARGETS):
@@ -522,15 +527,11 @@
 
     blocks = R // 8
     lax.fori_loop(0, blocks // 4, factor_block, 0)
-    wr1.wait_recv()
-    fr1 = start(weight_send(4, left, 1, 1))
-    wl0.wait_recv()
-    fl0 = start(weight_send(5, right, 0, 3))
 
     for d in range(X):
         yu[d].wait_recv()
     lax.fori_loop(0, quarter // 32, choose_rows, 0)
-    for copy in (wr0, wl1, fr1, fl0):
+    for copy in shares:
         copy.wait_recv()
     for d in (1, 2, 3):
         who = lax.rem(x + d, X)

time: 110 us -> 110 us (level)
  no operation moved by 1% of the time
where the time goes in v5:
time: 110 us; the launch traced here: 108 us
  Pallas kernels  105 us (95%)
  local copies, waits for them, and re-layouts  2.26 us (2%)
    pallas_call x1, Pallas kernels, on_device(): pl.pallas_call(functools.partial(kernel, rows, layers, tile), out_shape=(...  105 us
    unnamed x4, local copies, waits for them, and re-layouts  2.26 us

profile of v5, /device:TPU:6, one launch (start us, length us, event | category | flops | bytes accessed | tf_op | source)
XLA Modules:
  0.0 108.4 jit_solution(8890900525502880187)
XLA Ops:
  0.6 105.5 %trailing_update.1 = (f32[1,128,2,128]{3,2,1,0:T(2,128)}, f32[1,128,2,128]{3,2,1,0:T(2,128)}) custom-call(bf16[1,2,2048,128]{3,2,1,0:T(8,128)(2,1)} %u_hbm.1, bf16[1,2,2048,128]{3,2,1,0:T(8,128)(2,1)} %v_hbm.1, bf16[2048,128]{1,0:T(8,128)(2,1)} %test_hbm.1, s32[1,2]{1,0:T(1,128)} %ranks_hbm.1, s32[1,2]{1,0:T(1,128)} %offs_hbm.1), custom_call_target="tpu_custom_call" | custom-call | tf_op jit(solution)/shard_map/trailing_update/pallas_call | solution.py:639
  106.1 0.0 copy-start
  106.1 1.6 %copy.9 = f32[1,128,2,128]{3,2,1,0:T(2,128)} copy(f32[1,128,2,128]{3,2,1,0:T(2,128)} %get-tuple-element.4) | data formatting | bytes 262144
  107.7 0.0 copy-done
  107.7 0.7 copy.10
Async XLA Ops:
  106.1 1.6 %copy-start = (f32[1,128,2,128]{3,2,1,0:T(2,128)S(1)}, f32[1,128,2,128]{3,2,1,0:T(2,128)}, u32[]{:S(2)}) copy-start(f32[1,128,2,128]{3,2,1,0:T(2,128)} %get-tuple-element.5) | copy-start | bytes 393220
